TPU v7x, 256 devices: a whole 4x4x8 slice. The times are simulated.
256 devices in a mesh: users: 32 (over x, z_hi, core), ctx: 8 (over y, z_lo).
Axes of the slice: x: 4, y: 4, z: 8 (z_hi: 4, z_lo: 2; z = z_hi * 2 + z_lo), core: 2. Of those that a mesh axis runs over, the one named last changes fastest.
Arguments:
- event_embed: bfloat16 [512, 32, 8192], P(('users', 'ctx')), may hold values from -6 to 6
- event_time_bucket: int32 [32, 8192], P('users', 'ctx'), may hold values from 0 to 127
- time_table: float32 [128, 512], replicated, may hold values from -6 to 6
- history_length: int32 [32], P('users'), may hold values from 2048 to 8192, as said below
- w_proj: bfloat16 [512, 2048], replicated, may hold values from -0.25 to 0.25
- w_out: bfloat16 [512, 512], replicated, may hold values from -0.25 to 0.25
Outputs:
- layer_out: bfloat16 [32, 8192, 512], P('users', 'ctx')
Inputs may be any that keep to these rules, and one draw needn't show every extreme that they name: `history_length`: one user in every draw has a full history of 8192 events.
All inputs are finite; a program needn't handle non-finite values.
Results may differ from a plain program's by a relative error of at most 0.0068.
Values may be sent and summed in bfloat16 or wider, within the bound.
No kernel may reach another device: no remote copies, remote signals or barrier semaphores. Data moves between devices by JAX's collectives and lax.ppermute only.
A program may use at most 64 MiB of HBM per device.

v0:
```python
import jax
import jax.numpy as jnp
from jax import lax
from jax.experimental import pallas as pl
from jax.experimental.pallas import tpu as pltpu
from jax.sharding import PartitionSpec as P

H = 8
HEAD = 64
BAND = 512
PREFIX = 512
D = 512
L = 1024
PAIR = 128
PAIRS = D // PAIR
TILE = 256
BLK = 128
VMEM_LIMIT = 56 * 1024 * 1024
F32 = jnp.float32
BF16 = jnp.bfloat16


def silu_of_half(h):
    return h * jnp.tanh(h) + h


def dot(a, b, dims):
    return lax.dot_general(a, b, (dims, ((), ())), preferred_element_type=F32)


def pack_kernel(x_ref, out_ref, rows, prefix_rows):
    users = x_ref.shape[1]
    blocks = x_ref.shape[2] // BLK
    ctx = out_ref.shape[0] // users
    for k in range(2):
        for u in range(0, users, 16):
            for t in range(blocks):
                part = x_ref[k, u : u + 16, t * BLK : (t + 1) * BLK].astype(F32)
                rows[pl.ds((k * users + u) * blocks + t, 16, stride=blocks), :] = part
                if t < 4:
                    prefix_rows[pl.ds(u * 8 + k * 4 + t, 16, stride=8), :] = part

    def user(u, _):
        head = prefix_rows[pl.ds(pl.multiple_of(u * 8, 8), 8), :]
        for c in range(ctx):
            first = rows[pl.ds(pl.multiple_of(u * blocks + c * 8, 8), 8), :]
            second = rows[pl.ds(pl.multiple_of((users + u) * blocks + c * 8, 8), 8), :]
            out_ref[u * ctx + c] = jnp.concatenate([first, second, head], axis=0).astype(BF16)
        return 0

    lax.fori_loop(0, users, user, 0, unroll=2)


def pack(x, ctx):
    users, events = x.shape[1], x.shape[2]
    return pl.pallas_call(
        pack_kernel,
        out_shape=jax.ShapeDtypeStruct((users * ctx, 24, BLK), BF16),
        in_specs=[pl.BlockSpec(memory_space=pltpu.VMEM)],
        out_specs=pl.BlockSpec(memory_space=pltpu.VMEM),
        scratch_shapes=[
            pltpu.VMEM((2 * users * events // BLK, BLK), F32),
            pltpu.VMEM((users * 8, BLK), F32),
        ],
        compiler_params=pltpu.CompilerParams(vmem_limit_bytes=VMEM_LIMIT),
        name="pack",
    )(x)


def norm_kernel(r_ref, bucket_ref, head_bucket_ref, table_ref, low_ref, high_ref, head_ref, own, pre):
    sources = r_ref.shape[0]
    step = 32

    def widen(i, _):
        s = pl.multiple_of(i * step, step)
        part = r_ref[pl.ds(s, step)].astype(F32)
        own[pl.ds(pl.multiple_of(s * 16, 16 * step), 16 * step), :] = part[:, :16].reshape(16 * step, BLK)
        pre[pl.ds(pl.multiple_of(s * 8, 8 * step), 8 * step), :] = part[:, 16:].reshape(8 * step, BLK)
        return 0

    lax.fori_loop(0, sources // step, widen, 0)
    table = table_ref[...]
    t_hi = table.astype(BF16)
    rest = table - t_hi.astype(F32)
    t_mid = rest.astype(BF16)
    t_low = (rest - t_mid.astype(F32)).astype(BF16)
    parts = jnp.concatenate([t_hi, t_mid, t_low], axis=0)
    slot = lax.broadcasted_iota(jnp.int32, (table.shape[0], BLK), 0)

    def block(columns, buckets, out_ref, row):
        hot = (slot == buckets).astype(BF16)
        hot = jnp.concatenate([hot, hot, hot], axis=0)
        events = columns.T + dot(hot, parts, ((0,), (0,)))
        mean = jnp.sum(events * events, axis=1, keepdims=True) * (1.0 / D)
        out_ref[pl.ds(row, BLK), :] = (events * lax.rsqrt(mean + 1e-05)).astype(BF16)

    for j in (4, 5, 6, 7, 0, 1, 2, 3):
        block(
            own[pl.ds(j, D, stride=8), :],
            bucket_ref[:, j * BLK : (j + 1) * BLK],
            low_ref if j < 4 else high_ref,
            (j % 4) * BLK,
        )
    for j in range(4):
        block(pre[pl.ds(j, D, stride=4), :], head_bucket_ref[:, j * BLK : (j + 1) * BLK], head_ref, j * BLK)


def norm(r, bucket, head_bucket, table):
    half = jax.ShapeDtypeStruct((512, D), BF16)
    return pl.pallas_call(
        norm_kernel,
        out_shape=[half, half, half],
        in_specs=[pl.BlockSpec(memory_space=pltpu.VMEM)] * 4,
        out_specs=[pl.BlockSpec(memory_space=pltpu.VMEM)] * 3,
        scratch_shapes=[pltpu.VMEM((L * D // BLK, BLK), F32), pltpu.VMEM((PREFIX * D // BLK, BLK), F32)],
        compiler_params=pltpu.CompilerParams(vmem_limit_bytes=VMEM_LIMIT),
        name="norm",
    )(r, bucket, head_bucket, table)


def half_silu_proj(rows, weights):
    return silu_of_half(dot(rows, weights, ((1,), (0,))) * 0.5)


def head_masks():
    lane = lax.broadcasted_iota(jnp.int32, (TILE, PAIR), 1)
    return lane < HEAD


def finish(att, gating, scale, w_out):
    gated = (att * scale * gating.astype(F32)).astype(BF16)
    return dot(gated, w_out, ((1,), (0,))).astype(BF16)


def row_scale(first, length):
    pos = first + lax.broadcasted_iota(jnp.int32, (TILE, 1), 0)
    count = jnp.minimum(pos + 1, BAND + PREFIX).astype(F32)
    return jnp.where(pos < length, 1.0 / count, 0.0)


def main_kernel(
    place_ref, low_ref, high_ref, head_ref, w_ref, w_out_ref,
    out_ref, acc_ref, query_ref, gate_ref,
    keys, values, queries, gates, att,
):
    c = place_ref[0]
    length = place_ref[1]
    start = c * L

    for t in range(6):
        src = (head_ref, head_ref, low_ref, low_ref, high_ref, high_ref)[t]
        rows = src[(t % 2) * TILE : (t % 2 + 1) * TILE, :]
        at = slice(t * TILE, (t + 1) * TILE)
        v = half_silu_proj(rows, w_ref[:, D : 2 * D]).astype(BF16)
        k = half_silu_proj(rows, w_ref[:, 3 * D :]).astype(BF16)
        for p in range(PAIRS):
            values[p, at, :] = v[:, p * PAIR : (p + 1) * PAIR]
            keys[p, at, :] = k[:, p * PAIR : (p + 1) * PAIR]
        if t >= 2:
            own = slice((t - 2) * TILE, (t - 1) * TILE)
            q = (half_silu_proj(rows, w_ref[:, 2 * D : 3 * D]).astype(BF16) * 0.5).astype(BF16)
            for p in range(PAIRS):
                queries[p, own, :] = q[:, p * PAIR : (p + 1) * PAIR]
            g = half_silu_proj(rows, w_ref[:, :D]).astype(BF16)
            if t < 4:
                gate_ref[own, :] = g
            else:
                gates[(t - 4) * TILE : (t - 3) * TILE, :] = g

    first_head = head_masks()
    row = lax.broadcasted_iota(jnp.int32, (2 * TILE, TILE), 0)
    a = jnp.where(row < TILE, row, row - TILE)
    b = lax.broadcasted_iota(jnp.int32, (2 * TILE, TILE), 1)
    causal = b <= a
    lag = b - a

    def pair(p, _):
        for t in range(4):
            q = queries[p, t * TILE : (t + 1) * TILE, :]
            zero = jnp.zeros_like(q)
            qq = jnp.concatenate([jnp.where(first_head, q, zero), jnp.where(first_head, zero, q)], axis=0)
            total = jnp.zeros((2 * TILE, PAIR), F32)
            tiles = [("pre", 0), ("pre", 1)]
            if t >= 2:
                tiles.append(("far", t))
            if t >= 1:
                tiles.append(("mid", t + 1))
            tiles.append(("diag", t + 2))
            for kind, kt in tiles:
                at = slice(kt * TILE, (kt + 1) * TILE)
                s = dot(qq, keys[p, at, :], ((1,), (1,)))
                if kind == "diag":
                    s = jnp.where(causal, s, 0.0)
                elif kind == "far":
                    s = jnp.where(causal, 0.0, s)
                elif kind == "pre":
                    s = jnp.where(lag <= start + (t * TILE - BAND - kt * TILE), s, 0.0)
                w = silu_of_half(s).astype(BF16)
                total = total + dot(w, values[p, at, :], ((1,), (0,)))
            att[p, t * TILE : (t + 1) * TILE, :] = jnp.where(first_head, total[:TILE], total[TILE:])
        return 0

    lax.fori_loop(0, PAIRS, pair, 0)

    for p in range(PAIRS):
        acc_ref[p] = att[p, : 2 * TILE, :]
        query_ref[p] = queries[p, : 2 * TILE, :]
    for t in (2, 3):
        whole = jnp.concatenate([att[p, t * TILE : (t + 1) * TILE, :] for p in range(PAIRS)], axis=1)
        here = slice((t - 2) * TILE, (t - 1) * TILE)
        scale = row_scale(start + t * TILE, length)
        out_ref[here, :] = finish(whole, gates[here, :], scale, w_out_ref[...])


def main_part(place, low, high, head, w, w_out):
    vm = pl.BlockSpec(memory_space=pltpu.VMEM)
    return pl.pallas_call(
        main_kernel,
        grid=(1,),
        out_shape=[
            jax.ShapeDtypeStruct((L, D), BF16),
            jax.ShapeDtypeStruct((PAIRS, 512, PAIR), F32),
            jax.ShapeDtypeStruct((PAIRS, 512, PAIR), BF16),
            jax.ShapeDtypeStruct((512, D), BF16),
        ],
        in_specs=[pl.BlockSpec(memory_space=pltpu.SMEM)] + [vm] * 5,
        out_specs=[pl.BlockSpec((512, D), lambda i: (1, 0)), vm, vm, vm],
        scratch_shapes=[
            pltpu.VMEM((PAIRS, PREFIX + L, PAIR), BF16),
            pltpu.VMEM((PAIRS, PREFIX + L, PAIR), BF16),
            pltpu.VMEM((PAIRS, L, PAIR), BF16),
            pltpu.VMEM((512, D), BF16),
            pltpu.VMEM((PAIRS, L, PAIR), F32),
        ],
        compiler_params=pltpu.CompilerParams(vmem_limit_bytes=VMEM_LIMIT),
        cost_estimate=pl.CostEstimate(flops=20_000_000_000, bytes_accessed=8_000_000, transcendentals=0),
        name="main_part",
    )(place, low, high, head, w, w_out)


def edge_kernel(
    place_ref, edge_ref, w_ref, w_out_ref, acc_ref, query_ref, gate_ref, prev_ref,
    out_ref, keys, values,
):
    start = place_ref[0] * L
    length = place_ref[1]
    for t in range(2):
        at = slice(t * TILE, (t + 1) * TILE)
        rows = edge_ref[at, :]
        v = half_silu_proj(rows, w_ref[:, D : 2 * D]).astype(BF16)
        k = half_silu_proj(rows, w_ref[:, 3 * D :]).astype(BF16)
        for p in range(PAIRS):
            values[p, at, :] = v[:, p * PAIR : (p + 1) * PAIR]
            keys[p, at, :] = k[:, p * PAIR : (p + 1) * PAIR]
    first_head = head_masks()
    row = lax.broadcasted_iota(jnp.int32, (2 * TILE, TILE), 0)
    a = jnp.where(row < TILE, row, row - TILE)
    later = lax.broadcasted_iota(jnp.int32, (2 * TILE, TILE), 1) > a
    for t in range(2):
        here = slice(t * TILE, (t + 1) * TILE)
        columns = []
        for p in range(PAIRS):
            q = query_ref[p, here, :]
            zero = jnp.zeros_like(q)
            qq = jnp.concatenate([jnp.where(first_head, q, zero), jnp.where(first_head, zero, q)], axis=0)
            total = jnp.zeros((2 * TILE, PAIR), F32)
            for kt in range(t, 2):
                at = slice(kt * TILE, (kt + 1) * TILE)
                s = dot(qq, keys[p, at, :], ((1,), (1,)))
                if kt == t:
                    s = jnp.where(later, s, 0.0)
                w = silu_of_half(s).astype(BF16)
                total = total + dot(w, values[p, at, :], ((1,), (0,)))
            columns.append(acc_ref[p, here, :] + jnp.where(first_head, total[:TILE], total[TILE:]))
        whole = jnp.concatenate(columns, axis=1)
        out_ref[here, :] = finish(
            whole, gate_ref[here, :], row_scale(start + t * TILE, length), w_out_ref[...]
        )


def edge_part(place, edge, w, w_out, acc, query, gate, prev):
    vm = pl.BlockSpec(memory_space=pltpu.VMEM)
    return pl.pallas_call(
        edge_kernel,
        grid=(1,),
        out_shape=jax.ShapeDtypeStruct((L, D), BF16),
        in_specs=[pl.BlockSpec(memory_space=pltpu.SMEM)] + [vm] * 6 + [pl.BlockSpec(memory_space=pl.ANY)],
        out_specs=pl.BlockSpec((512, D), lambda i: (0, 0)),
        input_output_aliases={7: 0},
        scratch_shapes=[
            pltpu.VMEM((PAIRS, BAND, PAIR), BF16),
            pltpu.VMEM((PAIRS, BAND, PAIR), BF16),
        ],
        compiler_params=pltpu.CompilerParams(vmem_limit_bytes=VMEM_LIMIT),
        name="edge_part",
    )(place, edge, w, w_out, acc, query, gate, prev)


def local(event_embed, event_time_bucket, time_table, history_length, w_proj, w_out):
    ctx = lax.axis_size("ctx")
    c = lax.axis_index("ctx")
    place = jnp.stack([c.astype(jnp.int32), history_length[0]])
    head_bucket = lax.all_gather(event_time_bucket[:, :PREFIX], "ctx", axis=0)[0]
    sent = pack(event_embed, ctx)
    got = lax.all_to_all(sent, ("users", "ctx"), split_axis=0, concat_axis=0, tiled=True)
    low, high, head = norm(got, event_time_bucket, head_bucket, time_table)
    edge = lax.ppermute(high, "ctx", [(i, i + 1) for i in range(ctx - 1)])
    out, acc, query, gate = main_part(place, low, high, head, w_proj, w_out)
    out = edge_part(place, edge, w_proj, w_out, acc, query, gate, out)
    return out[None]


def solution(mesh):
    return jax.shard_map(
        local,
        mesh=mesh,
        in_specs=(P(("users", "ctx"), None, None), P("users", "ctx"), P(), P("users"), P(), P()),
        out_specs=P("users", "ctx", None),
        check_vma=False,
    )
```

profile of v0, /device:TPU:32, one launch (start us, length us, event | category | flops | bytes accessed | tf_op | source)
XLA Modules:
  0.0 108.8 jit_solution(2783588076848774930)
XLA Ops:
  0.0 4.3 %pack.1 = bf16[256,24,128]{2,1,0:T(8,128)(2,1)} custom-call(bf16[2,32,8192]{2,1,0:T(8,128)(2,1)} %x_ref.1), custom_call_target="tpu_custom_call" | custom-call | tf_op jit(solution)/shard_map/pack/pallas_call | solution.py:56
  4.3 0.0 copy-start.2
  4.3 14.4 %all-to-all-start = ((bf16[256,24,128]{2,1,0:T(8,128)(2,1)}), bf16[256,24,128]{2,1,0:T(8,128)(2,1)S(1)}, u32[]{:S(2)}, u32[]{:S(2)}) async-start(bf16[256,24,128]{2,1,0:T(8,128)(2,1)} %pack.1), calls=%async_computation | async-start | bytes 3145728 | tf_op jit(solution)/shard_map/all_to_all | solution.py:305
  19.4 0.0 copy-done.2
  19.4 51.7 %all-gather.1 = s32[8,1,512]{2,1,0:T(1,128)S(1)} all-gather(s32[1,1,512]{2,1,0:T(1,128)S(1)} %slice_bitcast_fusion.1), channel_id=2, replica_groups=mesh['users'=32,'ctx'=8] {'ctx'}, dimensions={0}, use_global_device_ids=true | all-gather | bytes 18432 | tf_op jit(solution)/shard_map/all_gather | solution.py:303
  71.1 0.6 pad_add_fusion.place_ref
  71.8 0.6 slice_bitcast_fusion.head_bucket_ref
  72.4 0.0 all-to-all-done.r_ref
  72.4 0.0 copy-start
  72.4 1.1 %copy-done = bf16[256,24,128]{2,1,0:T(8,128)(2,1)} copy-done((bf16[256,24,128]{2,1,0:T(8,128)(2,1)}, bf16[256,24,128]{2,1,0:T(8,128)(2,1)S(1)}, u32[]{:S(2)}) %copy-start) | copy-done | bytes 1572888
  73.5 4.5 %norm.1 = (bf16[512,512]{1,0:T(8,128)(2,1)}, bf16[512,512]{1,0:T(8,128)(2,1)}, bf16[512,512]{1,0:T(8,128)(2,1)}) custom-call(bf16[256,24,128]{2,1,0:T(8,128)(2,1)} %copy-done, s32[1,1024]{1,0:T(1,128)} %bucket_ref.1, s32[1,512]{1,0:T(1,128)} %slice_bitcast_fusion.head_bucket_ref, f32[128,512]{1,0:T(8,128)} %table_ref.1), custom_call_target="tpu_custom_call" | custom-call | tf_op jit(solution)/shard_map/norm/pallas_call | solution.py:110
  78.0 5.2 %collective-permute-start = (bf16[512,512]{1,0:T(8,128)(2,1)}, bf16[512,512]{1,0:T(8,128)(2,1)S(1)}, u32[]{:S(2)}, u32[]{:S(2)}) collective-permute-start(bf16[512,512]{1,0:T(8,128)(2,1)} %get-tuple-element.12.high_ref), channel_id=1, source_target_pairs={{0,1},{1,2},{2,3},{3,4},{4,5},{5,6},{6,7},{8,9},{9,10},{10,11},{11... | collective-permute-start | bytes 1572872 | tf_op jit(solution)/shard_map/ppermute | solution.py:307
  83.2 18.4 %main_part.1 = (bf16[1024,512]{1,0:T(8,128)(2,1)}, f32[4,512,128]{2,1,0:T(8,128)}, bf16[4,512,128]{2,1,0:T(8,128)(2,1)}, bf16[512,512]{1,0:T(8,128)(2,1)}) custom-call(s32[2]{0:T(128)} %pad_add_fusion.place_ref, bf16[512,512]{1,0:T(8,128)(2,1)} %get-tuple-element.13.low_ref, bf16[512,512]{1,0:T(8,128)(2,1)} %get-tuple-element.12.high_ref, ...), custom_call_target="tpu_custom_call" | custom-call | flops 20000000000 | bytes 8000000 | tf_op jit(solution)/shard_map/main_part/pallas_call | solution.py:217
  101.6 0.0 collective-permute-done.edge_ref
  101.6 0.0 copy-start.1
  101.7 0.8 copy-done.1
  102.4 6.4 %edge_part.1 = bf16[1024,512]{1,0:T(8,128)(2,1)} custom-call(s32[2]{0:T(128)} %pad_add_fusion.place_ref, bf16[512,512]{1,0:T(8,128)(2,1)} %copy-done.1, bf16[512,2048]{1,0:T(8,128)(2,1)} %w_ref.3, bf16[512,512]{1,0:T(8,128)(2,1)} %w_out_ref.3, f32[4,512,128]{2,1,0:T(8,128)} %get-tuple-element.15.acc_ref, ...), custom_call_target="tpu_custom_call", output_to_operand_aliasing={{}: (7, {})} | custom-call | tf_op jit(solution)/shard_map/edge_part/pallas_call | solution.py:283
  (1 shorter events, 0.0 us)
Async XLA Ops:
  4.3 15.0 %copy-start.2 = (s32[1,1024]{1,0:T(1,128)S(1)}, s32[1,1024]{1,0:T(1,128)}, u32[]{:S(2)}) copy-start(s32[1,1024]{1,0:T(1,128)} %bucket_ref.1) | copy-start | bytes 12292
  4.3 68.0 %all-to-all-start = ((bf16[256,24,128]{2,1,0:T(8,128)(2,1)}), bf16[256,24,128]{2,1,0:T(8,128)(2,1)S(1)}, u32[]{:S(2)}, u32[]{:S(2)}) async-start(bf16[256,24,128]{2,1,0:T(8,128)(2,1)} %pack.1), calls=%async_computation | async-start | bytes 3145728 | tf_op jit(solution)/shard_map/all_to_all | solution.py:305
  72.4 1.1 %copy-start = (bf16[256,24,128]{2,1,0:T(8,128)(2,1)}, bf16[256,24,128]{2,1,0:T(8,128)(2,1)S(1)}, u32[]{:S(2)}) copy-start(bf16[256,24,128]{2,1,0:T(8,128)(2,1)S(1)} %all-to-all-done.r_ref) | copy-start | bytes 4718596
  78.0 23.6 %collective-permute-start = (bf16[512,512]{1,0:T(8,128)(2,1)}, bf16[512,512]{1,0:T(8,128)(2,1)S(1)}, u32[]{:S(2)}, u32[]{:S(2)}) collective-permute-start(bf16[512,512]{1,0:T(8,128)(2,1)} %get-tuple-element.12.high_ref), channel_id=1, source_target_pairs={{0,1},{1,2},{2,3},{3,4},{4,5},{5,6},{6,7},{8,9},{9,10},{10,11},{11... | collective-permute-start | bytes 1572872 | tf_op jit(solution)/shard_map/ppermute | solution.py:307
  101.6 0.8 copy-start.1
where the time goes:
time: 109 us
  blocking collectives  51.7 us (47%)
  Pallas kernels  33.6 us (31%)
  starting transfers between devices  19.6 us (18%)
  local copies, waits for them, and re-layouts  2.52 us (2%)
    all_gather x1, blocking collectives, local(): lax.all_gather(event_time_bucket[:, :PREFIX], 'ctx', axis=0)[0]  51.7 us
    pallas_call x1, Pallas kernels, main_part(): pl.pallas_call(main_kernel, grid=(1,), out_shape=[jax.ShapeDtypeStruct((L...  18.4 us
    all_to_all x1, starting transfers between devices, local(): lax.all_to_all(sent, ('users', 'ctx'), split_axis=0, concat_axis=0, tiled...  14.4 us
    pallas_call x1, Pallas kernels, edge_part(): pl.pallas_call(edge_kernel, grid=(1,), out_shape=jax.ShapeDtypeStruct((L,...  6.36 us
    ppermute x1, starting transfers between devices, local(): edge = lax.ppermute(high, 'ctx', [(i, i + 1) for i in range(ctx - 1)])  5.21 us
    pallas_call x1, Pallas kernels, norm(): pl.pallas_call(norm_kernel, out_shape=[half, half, half], in_specs=[pl.Bl...  4.52 us
    pallas_call x1, Pallas kernels, pack(): pl.pallas_call(pack_kernel, out_shape=jax.ShapeDtypeStruct((users * ctx,...  4.34 us
  transfers between devices with their start and end apart: 2, of which 0 were waited for; matrix products, arithmetic and copies ran while one was open for 1% of the time, Pallas kernels for 17%

commit v1 on v0

v1 whole, which is shorter than its diff:
```python
import jax
import jax.numpy as jnp
from jax import lax
from jax.experimental import pallas as pl
from jax.experimental.pallas import tpu as pltpu
from jax.sharding import PartitionSpec as P

H = 8
HEAD = 64
BAND = 512
PREFIX = 512
D = 512
L = 1024
PAIR = 128
PAIRS = D // PAIR
TILE = 256
BLK = 128
VMEM_LIMIT = 32 * 1024 * 1024
F32 = jnp.float32
BF16 = jnp.bfloat16
VM = pl.BlockSpec(memory_space=pltpu.VMEM)


def silu_of_half(h):
    return h * jnp.tanh(h) + h


def dot(a, b, dims):
    return lax.dot_general(a, b, (dims, ((), ())), preferred_element_type=F32)


def pack_kernel(x_ref, out_ref, rows, head_rows):
    users = x_ref.shape[1]
    blocks = x_ref.shape[2] // BLK
    ctx = out_ref.shape[0] // users
    for k in range(2):
        for t in range(blocks):
            part = x_ref[k, :, t * BLK : (t + 1) * BLK].astype(F32)
            rows[pl.ds(k * users * blocks + t, users, stride=blocks), :] = part
            if t < 4:
                head_rows[pl.ds(k * 4 + t, users, stride=8), :] = part

    def user(u, _):
        head = head_rows[pl.ds(pl.multiple_of(u * 8, 8), 8), :]
        for c in range(ctx):
            first = rows[pl.ds(pl.multiple_of(u * blocks + c * 8, 8), 8), :]
            second = rows[pl.ds(pl.multiple_of((users + u) * blocks + c * 8, 8), 8), :]
            out_ref[u * ctx + c] = jnp.concatenate([first, second, head], axis=0).astype(BF16)
        return 0

    lax.fori_loop(0, users, user, 0, unroll=2)


def pack(x, ctx):
    users, events = x.shape[1], x.shape[2]
    part = 16
    return pl.pallas_call(
        pack_kernel,
        grid=(users // part,),
        out_shape=jax.ShapeDtypeStruct((users * ctx, 24, BLK), BF16),
        in_specs=[pl.BlockSpec((2, part, events), lambda i: (0, i, 0))],
        out_specs=pl.BlockSpec((part * ctx, 24, BLK), lambda i: (i, 0, 0)),
        scratch_shapes=[
            pltpu.VMEM((2 * part * events // BLK, BLK), F32),
            pltpu.VMEM((part * 8, BLK), F32),
        ],
        compiler_params=pltpu.CompilerParams(vmem_limit_bytes=VMEM_LIMIT),
        name="pack",
    )(x)


def time_parts(table):
    t_hi = table.astype(BF16)
    rest = table - t_hi.astype(F32)
    t_mid = rest.astype(BF16)
    t_low = (rest - t_mid.astype(F32)).astype(BF16)
    return jnp.concatenate([t_hi, t_mid, t_low], axis=0)


def normed(columns, hot, parts):
    hot = hot.astype(BF16)
    hot = jnp.concatenate([hot, hot, hot], axis=0)
    events = columns.T + dot(hot, parts, ((0,), (0,)))
    mean = jnp.sum(events * events, axis=1, keepdims=True) * (1.0 / D)
    return (events * lax.rsqrt(mean + 1e-05)).astype(BF16)


def norm_kernel(r_ref, bucket_ref, table_ref, low_ref, high_ref, pre_ref, own, raw, sem):
    sources = r_ref.shape[0]
    step = sources // 4
    copies = [
        pltpu.make_async_copy(r_ref.at[pl.ds(i * step, step)], raw.at[pl.ds(i * step, step)], sem.at[i])
        for i in range(4)
    ]
    for copy in copies:
        copy.start()
    parts = time_parts(table_ref[...])
    slot = lax.broadcasted_iota(jnp.int32, (table_ref.shape[0], BLK), 0)
    for i, copy in enumerate(copies):
        copy.wait()

        def widen(n, _):
            s = pl.multiple_of(i * step + n * 16, 16)
            part = raw[pl.ds(s, 16)].astype(F32)
            own[pl.ds(pl.multiple_of(s * 16, 256), 256), :] = part[:, :16].reshape(256, BLK)
            pre_ref[pl.ds(pl.multiple_of(s * 8, 128), 128), :] = part[:, 16:].reshape(128, BLK)
            return 0

        lax.fori_loop(0, step // 16, widen, 0)
    for j in (4, 5, 6, 7, 0, 1, 2, 3):
        hot = slot == bucket_ref[:, j * BLK : (j + 1) * BLK]
        out_ref = low_ref if j < 4 else high_ref
        out_ref[(j % 4) * BLK : (j % 4 + 1) * BLK, :] = normed(own[pl.ds(j, D, stride=8), :], hot, parts)


def norm(r, bucket, table):
    half = jax.ShapeDtypeStruct((512, D), BF16)
    return pl.pallas_call(
        norm_kernel,
        out_shape=[half, half, jax.ShapeDtypeStruct((PREFIX * D // BLK, BLK), F32)],
        in_specs=[pl.BlockSpec(memory_space=pl.ANY), VM, VM],
        out_specs=[VM] * 3,
        scratch_shapes=[
            pltpu.VMEM((L * D // BLK, BLK), F32),
            pltpu.VMEM(r.shape, BF16),
            pltpu.SemaphoreType.DMA((4,)),
        ],
        compiler_params=pltpu.CompilerParams(vmem_limit_bytes=VMEM_LIMIT),
        cost_estimate=pl.CostEstimate(flops=1_000_000_000, bytes_accessed=4_000_000, transcendentals=0),
        name="norm",
    )(r, bucket, table)


def store_pairs(ref, at, value):
    value = value.astype(BF16)
    for p in range(PAIRS):
        ref[p, at, :] = value[:, p * PAIR : (p + 1) * PAIR]


def half_silu_proj(rows, weights):
    return silu_of_half(dot(rows, weights, ((1,), (0,))) * 0.5)


def head_masks():
    lane = lax.broadcasted_iota(jnp.int32, (TILE, PAIR), 1)
    return lane < HEAD


def finish(att, gating, scale, w_out):
    gated = (att * scale * gating.astype(F32)).astype(BF16)
    return dot(gated, w_out, ((1,), (0,))).astype(BF16)


def row_scale(first, length):
    pos = first + lax.broadcasted_iota(jnp.int32, (TILE, 1), 0)
    count = jnp.minimum(pos + 1, BAND + PREFIX).astype(F32)
    return jnp.where(pos < length, 1.0 / count, 0.0)


def main_kernel(
    place_ref, low_ref, high_ref, pre_ref, table_ref, w_ref, w_out_ref, *refs,
):
    bucket_refs, refs = refs[: len(refs) - 11], refs[len(refs) - 11 :]
    out_ref, acc_ref, query_ref, gate_ref, keys, values, pre_keys, pre_values, queries, gates, att = refs
    c = place_ref[0]
    length = place_ref[1]
    start = c * L
    parts = time_parts(table_ref[...])
    slot = lax.broadcasted_iota(jnp.int32, (table_ref.shape[0], BLK), 0)
    buckets = bucket_refs[0][...]
    for ref in bucket_refs[1:]:
        buckets = buckets + ref[...]
    for t in range(2):
        rows = jnp.concatenate(
            [
                normed(pre_ref[pl.ds(j, D, stride=4), :], slot == buckets[:, j * BLK : (j + 1) * BLK], parts)
                for j in (2 * t, 2 * t + 1)
            ],
            axis=0,
        )
        at = slice(t * TILE, (t + 1) * TILE)
        store_pairs(pre_values, at, half_silu_proj(rows, w_ref[:, D : 2 * D]))
        store_pairs(pre_keys, at, half_silu_proj(rows, w_ref[:, 3 * D :]))

    for t in range(4):
        here = slice((t % 2) * TILE, (t % 2 + 1) * TILE)
        at = slice(t * TILE, (t + 1) * TILE)
        rows = (low_ref if t < 2 else high_ref)[here, :]
        store_pairs(values, at, half_silu_proj(rows, w_ref[:, D : 2 * D]))
        store_pairs(keys, at, half_silu_proj(rows, w_ref[:, 3 * D :]))
        store_pairs(queries, at, half_silu_proj(rows, w_ref[:, 2 * D : 3 * D]) * 0.5)
        (gate_ref if t < 2 else gates)[here, :] = half_silu_proj(rows, w_ref[:, :D]).astype(BF16)

    first_head = head_masks()
    row = lax.broadcasted_iota(jnp.int32, (2 * TILE, TILE), 0)
    a = jnp.where(row < TILE, row, row - TILE)
    b = lax.broadcasted_iota(jnp.int32, (2 * TILE, TILE), 1)
    causal = b <= a
    lag = b - a

    def pair(p, _):
        for t in range(4):
            q = queries[p, t * TILE : (t + 1) * TILE, :]
            zero = jnp.zeros_like(q)
            qq = jnp.concatenate([jnp.where(first_head, q, zero), jnp.where(first_head, zero, q)], axis=0)
            total = jnp.zeros((2 * TILE, PAIR), F32)
            tiles = [("pre", 0), ("pre", 1)]
            if t >= 2:
                tiles.append(("far", t - 2))
            if t >= 1:
                tiles.append(("mid", t - 1))
            tiles.append(("diag", t))
            for kind, kt in tiles:
                at = slice(kt * TILE, (kt + 1) * TILE)
                k_ref, v_ref = (pre_keys, pre_values) if kind == "pre" else (keys, values)
                s = dot(qq, k_ref[p, at, :], ((1,), (1,)))
                if kind == "diag":
                    s = jnp.where(causal, s, 0.0)
                elif kind == "far":
                    s = jnp.where(causal, 0.0, s)
                elif kind == "pre":
                    s = jnp.where(lag <= start + (t * TILE - BAND - kt * TILE), s, 0.0)
                w = silu_of_half(s).astype(BF16)
                total = total + dot(w, v_ref[p, at, :], ((1,), (0,)))
            att[p, t * TILE : (t + 1) * TILE, :] = jnp.where(first_head, total[:TILE], total[TILE:])
        return 0

    lax.fori_loop(0, PAIRS, pair, 0)

    for p in range(PAIRS):
        acc_ref[p] = att[p, : 2 * TILE, :]
        query_ref[p] = queries[p, : 2 * TILE, :]
    for t in (2, 3):
        whole = jnp.concatenate([att[p, t * TILE : (t + 1) * TILE, :] for p in range(PAIRS)], axis=1)
        here = slice((t - 2) * TILE, (t - 1) * TILE)
        scale = row_scale(start + t * TILE, length)
        out_ref[here, :] = finish(whole, gates[here, :], scale, w_out_ref[...])


def main_part(place, low, high, pre, table, w, w_out, buckets):
    return pl.pallas_call(
        main_kernel,
        grid=(1,),
        out_shape=[
            jax.ShapeDtypeStruct((L, D), BF16),
            jax.ShapeDtypeStruct((PAIRS, 512, PAIR), F32),
            jax.ShapeDtypeStruct((PAIRS, 512, PAIR), BF16),
            jax.ShapeDtypeStruct((512, D), BF16),
        ],
        in_specs=[pl.BlockSpec(memory_space=pltpu.SMEM)] + [VM] * (6 + len(buckets)),
        out_specs=[pl.BlockSpec((512, D), lambda i: (1, 0)), VM, VM, VM],
        scratch_shapes=[
            pltpu.VMEM((PAIRS, L, PAIR), BF16),
            pltpu.VMEM((PAIRS, L, PAIR), BF16),
            pltpu.VMEM((PAIRS, PREFIX, PAIR), BF16),
            pltpu.VMEM((PAIRS, PREFIX, PAIR), BF16),
            pltpu.VMEM((PAIRS, L, PAIR), BF16),
            pltpu.VMEM((512, D), BF16),
            pltpu.VMEM((PAIRS, L, PAIR), F32),
        ],
        compiler_params=pltpu.CompilerParams(vmem_limit_bytes=VMEM_LIMIT),
        cost_estimate=pl.CostEstimate(flops=20_000_000_000, bytes_accessed=8_000_000, transcendentals=0),
        name="main_part",
    )(place, low, high, pre, table, w, w_out, *buckets)


def edge_kernel(
    place_ref, edge_ref, w_ref, w_out_ref, acc_ref, query_ref, gate_ref, prev_ref,
    out_ref, keys, values,
):
    start = place_ref[0] * L
    length = place_ref[1]
    for t in range(2):
        at = slice(t * TILE, (t + 1) * TILE)
        rows = edge_ref[at, :]
        store_pairs(values, at, half_silu_proj(rows, w_ref[:, D : 2 * D]))
        store_pairs(keys, at, half_silu_proj(rows, w_ref[:, 3 * D :]))
    first_head = head_masks()
    row = lax.broadcasted_iota(jnp.int32, (2 * TILE, TILE), 0)
    a = jnp.where(row < TILE, row, row - TILE)
    later = lax.broadcasted_iota(jnp.int32, (2 * TILE, TILE), 1) > a
    for t in range(2):
        here = slice(t * TILE, (t + 1) * TILE)
        columns = []
        for p in range(PAIRS):
            q = query_ref[p, here, :]
            zero = jnp.zeros_like(q)
            qq = jnp.concatenate([jnp.where(first_head, q, zero), jnp.where(first_head, zero, q)], axis=0)
            total = jnp.zeros((2 * TILE, PAIR), F32)
            for kt in range(t, 2):
                at = slice(kt * TILE, (kt + 1) * TILE)
                s = dot(qq, keys[p, at, :], ((1,), (1,)))
                if kt == t:
                    s = jnp.where(later, s, 0.0)
                w = silu_of_half(s).astype(BF16)
                total = total + dot(w, values[p, at, :], ((1,), (0,)))
            columns.append(acc_ref[p, here, :] + jnp.where(first_head, total[:TILE], total[TILE:]))
        whole = jnp.concatenate(columns, axis=1)
        out_ref[here, :] = finish(
            whole, gate_ref[here, :], row_scale(start + t * TILE, length), w_out_ref[...]
        )


def edge_part(place, edge, w, w_out, acc, query, gate, prev):
    return pl.pallas_call(
        edge_kernel,
        grid=(1,),
        out_shape=jax.ShapeDtypeStruct((L, D), BF16),
        in_specs=[pl.BlockSpec(memory_space=pltpu.SMEM)] + [VM] * 6 + [pl.BlockSpec(memory_space=pl.ANY)],
        out_specs=pl.BlockSpec((512, D), lambda i: (0, 0)),
        input_output_aliases={7: 0},
        scratch_shapes=[
            pltpu.VMEM((PAIRS, BAND, PAIR), BF16),
            pltpu.VMEM((PAIRS, BAND, PAIR), BF16),
        ],
        compiler_params=pltpu.CompilerParams(vmem_limit_bytes=VMEM_LIMIT),
        name="edge_part",
    )(place, edge, w, w_out, acc, query, gate, prev)


def local(event_embed, event_time_bucket, time_table, history_length, w_proj, w_out):
    ctx = lax.axis_size("ctx")
    c = lax.axis_index("ctx").astype(jnp.int32)
    place = jnp.stack([c, history_length[0]])
    first = event_time_bucket[:, :PREFIX]
    buckets = [jnp.where(c == 0, first, 0)] + [lax.ppermute(first, "ctx", [(0, k)]) for k in range(1, ctx)]
    got = lax.all_to_all(pack(event_embed, ctx), ("users", "ctx"), split_axis=0, concat_axis=0, tiled=True)
    low, high, pre = norm(got, event_time_bucket, time_table)
    edge = lax.ppermute(high, "ctx", [(i, i + 1) for i in range(ctx - 1)])
    out, acc, query, gate = main_part(place, low, high, pre, time_table, w_proj, w_out, buckets)
    out = edge_part(place, edge, w_proj, w_out, acc, query, gate, out)
    return out[None]


def solution(mesh):
    return jax.shard_map(
        local,
        mesh=mesh,
        in_specs=(P(("users", "ctx"), None, None), P("users", "ctx"), P(), P("users"), P(), P()),
        out_specs=P("users", "ctx", None),
        check_vma=False,
    )
```

time: 109 us -> 90.2 us (0.83)
  blocking collectives: 51.7 us -> 0 us
  waiting for transfers between devices: 0.01 us -> 34.8 us
  Pallas kernels: 33.6 us -> 27.4 us
  starting transfers between devices: 19.6 us -> 24.6 us
  local copies, waits for them, and re-layouts: 2.52 us -> 1.24 us
    all_gather x1 -> x0, blocking collectives: 51.7 us -> none  [local(): lax.all_gather(event_time_bucket[:, :PREFIX], 'ctx', axis=0)[0]]
    ppermute x0 -> x7, waiting for transfers between devices: none -> 24.3 us  [local(): lax.ppermute(first, 'ctx', [(0, k)])]
    all_to_all x1, waiting for transfers between devices: 0.01 us -> 10.5 us  [local(): lax.all_to_all(pack(event_embed, ctx), ('users', 'ctx'), split_axis=0, co...]
    ppermute x0 -> x7, starting transfers between devices: none -> 5.25 us  [local(): lax.ppermute(first, 'ctx', [(0, k)])]
    pallas_call x2, Pallas kernels: 8.86 us -> 5.67 us  [the longest x1 3 us: pack(): pl.pallas_call(pack_kernel, grid=(users // part,), out_shape=jax.ShapeDty...]
    pallas_call x1, Pallas kernels: 6.36 us -> 4.52 us  [edge_part(): pl.pallas_call(edge_kernel, grid=(1,), out_shape=jax.ShapeDtypeStruct((L,...]
    pallas_call x1, Pallas kernels: 18.4 us -> 17.2 us  [main_part(): pl.pallas_call(main_kernel, grid=(1,), out_shape=[jax.ShapeDtypeStruct((L...]
    ppermute x1, starting transfers between devices: 5.21 us -> 4.12 us  [local(): edge = lax.ppermute(high, 'ctx', [(i, i + 1) for i in range(ctx - 1)])]
  transfers between devices with their start and end apart: 2 -> 9, of which waited for: 0 -> 2; matrix products, arithmetic and copies ran while one was open for 1% -> 0% of each run, Pallas kernels for 17% -> 22%
where the time goes in v1:
time: 90.2 us; the launch traced here: 89 us
  waiting for transfers between devices  34.8 us (39%)
  Pallas kernels  27.4 us (30%)
  starting transfers between devices  24.6 us (27%)
  local copies, waits for them, and re-layouts  1.24 us (1%)
    ppermute x7, waiting for transfers between devices, local(): lax.ppermute(first, 'ctx', [(0, k)])  24.3 us
    pallas_call x1, Pallas kernels, main_part(): pl.pallas_call(main_kernel, grid=(1,), out_shape=[jax.ShapeDtypeStruct((L...  17.2 us
    all_to_all x1, starting transfers between devices, local(): lax.all_to_all(pack(event_embed, ctx), ('users', 'ctx'), split_axis=0, co...  15.3 us
    all_to_all x1, waiting for transfers between devices, local(): lax.all_to_all(pack(event_embed, ctx), ('users', 'ctx'), split_axis=0, co...  10.5 us
    ppermute x7, starting transfers between devices, local(): lax.ppermute(first, 'ctx', [(0, k)])  5.25 us
    pallas_call x1, Pallas kernels, edge_part(): pl.pallas_call(edge_kernel, grid=(1,), out_shape=jax.ShapeDtypeStruct((L,...  4.52 us
    ppermute x1, starting transfers between devices, local(): edge = lax.ppermute(high, 'ctx', [(i, i + 1) for i in range(ctx - 1)])  4.12 us
    pallas_call x1, Pallas kernels, pack(): pl.pallas_call(pack_kernel, grid=(users // part,), out_shape=jax.ShapeDty...  3 us
  transfers between devices with their start and end apart: 9, of which 2 were waited for; matrix products, arithmetic and copies ran while one was open for 0% of the time, Pallas kernels for 22%

profile of v1, /device:TPU:32, one launch (start us, length us, event | category | flops | bytes accessed | tf_op | source)
XLA Modules:
  0.0 89.0 jit_solution(2923852098843371267)
XLA Ops:
  0.0 0.0 copy-start.1
  0.0 1.2 %copy-done.1 = bf16[2,32,8192]{2,1,0:T(8,128)(2,1)S(1)} copy-done((bf16[2,32,8192]{2,1,0:T(8,128)(2,1)S(1)}, bf16[2,32,8192]{2,1,0:T(8,128)(2,1)}, u32[]{:S(2)}) %copy-start.1) | copy-done | bytes 1048600
  1.2 3.0 %pack.1 = bf16[256,24,128]{2,1,0:T(8,128)(2,1)} custom-call(bf16[2,32,8192]{2,1,0:T(8,128)(2,1)S(1)} %copy-done.1), custom_call_target="tpu_custom_call" | custom-call | tf_op jit(solution)/shard_map/pack/pallas_call | solution.py:57
  4.2 0.0 copy-start.3
  4.2 0.0 copy-start.4
  4.2 15.3 %all-to-all-start = ((bf16[256,24,128]{2,1,0:T(8,128)(2,1)}), bf16[256,24,128]{2,1,0:T(8,128)(2,1)}, u32[]{:S(2)}, u32[]{:S(2)}) async-start(bf16[256,24,128]{2,1,0:T(8,128)(2,1)} %pack.1), calls=%async_computation | async-start | bytes 3145728 | tf_op jit(solution)/shard_map/all_to_all | solution.py:327
  19.5 0.0 copy-done.3
  19.5 1.3 %collective-permute-start.1 = (s32[1,512]{1,0:T(1,128)S(1)}, s32[1,512]{1,0:T(1,128)S(1)}, u32[]{:S(2)}, u32[]{:S(2)}) collective-permute-start(s32[1,512]{1,0:T(1,128)S(1)} %get-tuple-element.19), channel_id=1, source_target_pairs={{0,1},{8,9},{16,17},{24,25},{32,33},{40,41},{48,49},{56,57},{64,65... | collective-permute-start | bytes 6152 | tf_op jit(solution)/shard_map/ppermute | solution.py:326
  20.8 0.7 collective-permute-start.2
  21.5 0.7 collective-permute-start.3
  22.2 0.7 collective-permute-start.4
  22.8 0.7 collective-permute-start.5
  24.2 0.1 pad_add_fusion.place_ref
  24.2 0.0 copy-start
  24.2 0.0 copy-start.2
  24.2 24.3 %collective-permute-done.1.refs_1_ = s32[1,512]{1,0:T(1,128)S(1)} collective-permute-done((s32[1,512]{1,0:T(1,128)S(1)}, s32[1,512]{1,0:T(1,128)S(1)}, u32[]{:S(2)}, u32[]{:S(2)}) %collective-permute-start.1) | collective-permute-done | bytes 2080 | tf_op jit(solution)/shard_map/ppermute | solution.py:326
  48.5 0.7 collective-permute-start.6
  49.2 0.0 collective-permute-done.2.refs_2_
  49.2 0.7 collective-permute-start.7
  49.9 10.5 %all-to-all-done.r_ref = bf16[256,24,128]{2,1,0:T(8,128)(2,1)} async-done(((bf16[256,24,128]{2,1,0:T(8,128)(2,1)}), bf16[256,24,128]{2,1,0:T(8,128)(2,1)}, u32[]{:S(2)}, u32[]{:S(2)}) %all-to-all-start) | async-done | bytes 1572896 | tf_op jit(solution)/shard_map/all_to_all | solution.py:327
  60.4 0.0 copy-done.4
  60.4 2.7 %norm.1 = (bf16[512,512]{1,0:T(8,128)(2,1)S(1)}, bf16[512,512]{1,0:T(8,128)(2,1)S(1)}, f32[2048,128]{1,0:T(8,128)S(1)}) custom-call(bf16[256,24,128]{2,1,0:T(8,128)(2,1)} %all-to-all-done.r_ref, s32[1,1024]{1,0:T(1,128)S(1)} %copy-done.3, f32[128,512]{1,0:T(8,128)S(1)} %copy-done.4), custom_call_target="tpu_custom_call" | custom-call | flops 1000000000 | bytes 4000000 | tf_op jit(solution)/shard_map/norm/pallas_call | solution.py:118
  63.0 0.0 collective-permute-done.3.refs_3_
  63.1 4.1 %collective-permute-start = (bf16[512,512]{1,0:T(8,128)(2,1)S(1)}, bf16[512,512]{1,0:T(8,128)(2,1)S(1)}, u32[]{:S(2)}, u32[]{:S(2)}) collective-permute-start(bf16[512,512]{1,0:T(8,128)(2,1)S(1)} %get-tuple-element.12.high_ref), channel_id=1, source_target_pairs={{0,1},{1,2},{2,3},{3,4},{4,5},{5,6},{6,7},{8,9},{9,10},{10,11},{11... | collective-permute-start | bytes 1572872 | tf_op jit(solution)/shard_map/ppermute | solution.py:329
  67.2 0.0 collective-permute-done.4.refs_4_
  67.2 0.0 collective-permute-done.5.refs_5_
  67.2 0.0 collective-permute-done.6.refs_6_
  67.2 0.0 collective-permute-done.7.refs_7_
  67.2 0.0 copy-done
  67.2 0.0 copy-done.2
  67.2 17.2 %main_part.1 = (bf16[1024,512]{1,0:T(8,128)(2,1)}, f32[4,512,128]{2,1,0:T(8,128)S(1)}, bf16[4,512,128]{2,1,0:T(8,128)(2,1)S(1)}, bf16[512,512]{1,0:T(8,128)(2,1)S(1)}) custom-call(s32[2]{0:T(128)S(1)} %pad_add_fusion.place_ref, bf16[512,512]{1,0:T(8,128)(2,1)S(1)} %get-tuple-element.13.low_ref, bf16[512,512]{1,0:T(8,128)(2,1)S(1)} %get-tuple-element.12.high_ref, ...), custom_call_target="tpu_custom_call" | custom-call | flops 20000000000 | bytes 8000000 | tf_op jit(solution)/shard_map/main_part/pallas_call | solution.py:241
  84.4 0.0 collective-permute-done.edge_ref
  84.4 4.5 %edge_part.1 = bf16[1024,512]{1,0:T(8,128)(2,1)} custom-call(s32[2]{0:T(128)S(1)} %pad_add_fusion.place_ref, bf16[512,512]{1,0:T(8,128)(2,1)S(1)} %collective-permute-done.edge_ref, bf16[512,2048]{1,0:T(8,128)(2,1)S(1)} %copy-done, bf16[512,512]{1,0:T(8,128)(2,1)S(1)} %copy-done.2, ...), custom_call_target="tpu_custom_call", output_to_operand_aliasing={{}: (7, {})} | custom-call | tf_op jit(solution)/shard_map/edge_part/pallas_call | solution.py:305
  (1 shorter events, 0.0 us)
Async XLA Ops:
  0.0 1.2 %copy-start.1 = (bf16[2,32,8192]{2,1,0:T(8,128)(2,1)S(1)}, bf16[2,32,8192]{2,1,0:T(8,128)(2,1)}, u32[]{:S(2)}) copy-start(bf16[2,32,8192]{2,1,0:T(8,128)(2,1)} %x_ref.1) | copy-start | bytes 3145732
  4.2 15.3 %copy-start.3 = (s32[1,1024]{1,0:T(1,128)S(1)}, s32[1,1024]{1,0:T(1,128)}, u32[]{:S(2)}) copy-start(s32[1,1024]{1,0:T(1,128)} %bucket_ref.1) | copy-start | bytes 12292
  4.2 56.1 %copy-start.4 = (f32[128,512]{1,0:T(8,128)S(1)}, f32[128,512]{1,0:T(8,128)}, u32[]{:S(2)}) copy-start(f32[128,512]{1,0:T(8,128)} %table_ref.3) | copy-start | bytes 786436
  4.2 56.1 %all-to-all-start = ((bf16[256,24,128]{2,1,0:T(8,128)(2,1)}), bf16[256,24,128]{2,1,0:T(8,128)(2,1)}, u32[]{:S(2)}, u32[]{:S(2)}) async-start(bf16[256,24,128]{2,1,0:T(8,128)(2,1)} %pack.1), calls=%async_computation | async-start | bytes 3145728 | tf_op jit(solution)/shard_map/all_to_all | solution.py:327
  19.5 29.0 %collective-permute-start.1 = (s32[1,512]{1,0:T(1,128)S(1)}, s32[1,512]{1,0:T(1,128)S(1)}, u32[]{:S(2)}, u32[]{:S(2)}) collective-permute-start(s32[1,512]{1,0:T(1,128)S(1)} %get-tuple-element.19), channel_id=1, source_target_pairs={{0,1},{8,9},{16,17},{24,25},{32,33},{40,41},{48,49},{56,57},{64,65... | collective-permute-start | bytes 6152 | tf_op jit(solution)/shard_map/ppermute | solution.py:326
  20.8 28.4 %collective-permute-start.2 = (s32[1,512]{1,0:T(1,128)S(1)}, s32[1,512]{1,0:T(1,128)S(1)}, u32[]{:S(2)}, u32[]{:S(2)}) collective-permute-start(s32[1,512]{1,0:T(1,128)S(1)} %get-tuple-element.19), channel_id=1, source_target_pairs={{0,2},{8,10},{16,18},{24,26},{32,34},{40,42},{48,50},{56,58},{64,6... | collective-permute-start | bytes 6152 | tf_op jit(solution)/shard_map/ppermute | solution.py:326
  21.5 41.5 %collective-permute-start.3 = (s32[1,512]{1,0:T(1,128)S(1)}, s32[1,512]{1,0:T(1,128)S(1)}, u32[]{:S(2)}, u32[]{:S(2)}) collective-permute-start(s32[1,512]{1,0:T(1,128)S(1)} %get-tuple-element.19), channel_id=1, source_target_pairs={{0,3},{8,11},{16,19},{24,27},{32,35},{40,43},{48,51},{56,59},{64,6... | collective-permute-start | bytes 6152 | tf_op jit(solution)/shard_map/ppermute | solution.py:326
  22.2 45.0 %collective-permute-start.4 = (s32[1,512]{1,0:T(1,128)S(1)}, s32[1,512]{1,0:T(1,128)S(1)}, u32[]{:S(2)}, u32[]{:S(2)}) collective-permute-start(s32[1,512]{1,0:T(1,128)S(1)} %get-tuple-element.19), channel_id=1, source_target_pairs={{0,4},{8,12},{16,20},{24,28},{32,36},{40,44},{48,52},{56,60},{64,6... | collective-permute-start | bytes 6152 | tf_op jit(solution)/shard_map/ppermute | solution.py:326
  22.8 44.4 %collective-permute-start.5 = (s32[1,512]{1,0:T(1,128)S(1)}, s32[1,512]{1,0:T(1,128)S(1)}, u32[]{:S(2)}, u32[]{:S(2)}) collective-permute-start(s32[1,512]{1,0:T(1,128)S(1)} %get-tuple-element.19), channel_id=1, source_target_pairs={{0,5},{8,13},{16,21},{24,29},{32,37},{40,45},{48,53},{56,61},{64,6... | collective-permute-start | bytes 6152 | tf_op jit(solution)/shard_map/ppermute | solution.py:326
  24.2 43.0 %copy-start = (bf16[512,2048]{1,0:T(8,128)(2,1)S(1)}, bf16[512,2048]{1,0:T(8,128)(2,1)}, u32[]{:S(2)}) copy-start(bf16[512,2048]{1,0:T(8,128)(2,1)} %w_ref.3) | copy-start | bytes 6291460
  24.2 43.0 %copy-start.2 = (bf16[512,512]{1,0:T(8,128)(2,1)S(1)}, bf16[512,512]{1,0:T(8,128)(2,1)}, u32[]{:S(2)}) copy-start(bf16[512,512]{1,0:T(8,128)(2,1)} %w_out_ref.3) | copy-start | bytes 1572868
  48.5 18.7 %collective-permute-start.6 = (s32[1,512]{1,0:T(1,128)S(1)}, s32[1,512]{1,0:T(1,128)S(1)}, u32[]{:S(2)}, u32[]{:S(2)}) collective-permute-start(s32[1,512]{1,0:T(1,128)S(1)} %get-tuple-element.19), channel_id=1, source_target_pairs={{0,6},{8,14},{16,22},{24,30},{32,38},{40,46},{48,54},{56,62},{64,7... | collective-permute-start | bytes 6152 | tf_op jit(solution)/shard_map/ppermute | solution.py:326
  49.2 18.0 %collective-permute-start.7 = (s32[1,512]{1,0:T(1,128)S(1)}, s32[1,512]{1,0:T(1,128)S(1)}, u32[]{:S(2)}, u32[]{:S(2)}) collective-permute-start(s32[1,512]{1,0:T(1,128)S(1)} %get-tuple-element.19), channel_id=1, source_target_pairs={{0,7},{8,15},{16,23},{24,31},{32,39},{40,47},{48,55},{56,63},{64,7... | collective-permute-start | bytes 6152 | tf_op jit(solution)/shard_map/ppermute | solution.py:326
  63.1 21.4 %collective-permute-start = (bf16[512,512]{1,0:T(8,128)(2,1)S(1)}, bf16[512,512]{1,0:T(8,128)(2,1)S(1)}, u32[]{:S(2)}, u32[]{:S(2)}) collective-permute-start(bf16[512,512]{1,0:T(8,128)(2,1)S(1)} %get-tuple-element.12.high_ref), channel_id=1, source_target_pairs={{0,1},{1,2},{2,3},{3,4},{4,5},{5,6},{6,7},{8,9},{9,10},{10,11},{11... | collective-permute-start | bytes 1572872 | tf_op jit(solution)/shard_map/ppermute | solution.py:329

commit v2 on v1

--- a/solution.py
+++ b/solution.py
@@ -16,6 +16,7 @@
 TILE = 256
 BLK = 128
 VMEM_LIMIT = 32 * 1024 * 1024
+PACK_LIMIT = 60 * 1024 * 1024
 F32 = jnp.float32
 BF16 = jnp.bfloat16
 VM = pl.BlockSpec(memory_space=pltpu.VMEM)
@@ -64,7 +65,7 @@
             pltpu.VMEM((2 * part * events // BLK, BLK), F32),
             pltpu.VMEM((part * 8, BLK), F32),
         ],
-        compiler_params=pltpu.CompilerParams(vmem_limit_bytes=VMEM_LIMIT),
+        compiler_params=pltpu.CompilerParams(vmem_limit_bytes=PACK_LIMIT),
         name="pack",
     )(x)
 
@@ -129,6 +130,12 @@
         cost_estimate=pl.CostEstimate(flops=1_000_000_000, bytes_accessed=4_000_000, transcendentals=0),
         name="norm",
     )(r, bucket, table)
+
+
+def store_turned(ref, at, value):
+    turned = value.astype(BF16).T
+    for p in range(PAIRS):
+        ref[p, :, at] = turned[p * PAIR : (p + 1) * PAIR, :]
 
 
 def store_pairs(ref, at, value):
@@ -180,14 +187,14 @@
         )
         at = slice(t * TILE, (t + 1) * TILE)
         store_pairs(pre_values, at, half_silu_proj(rows, w_ref[:, D : 2 * D]))
-        store_pairs(pre_keys, at, half_silu_proj(rows, w_ref[:, 3 * D :]))
+        store_turned(pre_keys, at, half_silu_proj(rows, w_ref[:, 3 * D :]))
 
     for t in range(4):
         here = slice((t % 2) * TILE, (t % 2 + 1) * TILE)
         at = slice(t * TILE, (t + 1) * TILE)
         rows = (low_ref if t < 2 else high_ref)[here, :]
         store_pairs(values, at, half_silu_proj(rows, w_ref[:, D : 2 * D]))
-        store_pairs(keys, at, half_silu_proj(rows, w_ref[:, 3 * D :]))
+        store_turned(keys, at, half_silu_proj(rows, w_ref[:, 3 * D :]))
         store_pairs(queries, at, half_silu_proj(rows, w_ref[:, 2 * D : 3 * D]) * 0.5)
         (gate_ref if t < 2 else gates)[here, :] = half_silu_proj(rows, w_ref[:, :D]).astype(BF16)
 
@@ -199,33 +206,39 @@
     lag = b - a
 
     def pair(p, _):
+        stack = []
         for t in range(4):
             q = queries[p, t * TILE : (t + 1) * TILE, :]
             zero = jnp.zeros_like(q)
-            qq = jnp.concatenate([jnp.where(first_head, q, zero), jnp.where(first_head, zero, q)], axis=0)
-            total = jnp.zeros((2 * TILE, PAIR), F32)
-            tiles = [("pre", 0), ("pre", 1)]
-            if t >= 2:
-                tiles.append(("far", t - 2))
-            if t >= 1:
-                tiles.append(("mid", t - 1))
-            tiles.append(("diag", t))
-            for kind, kt in tiles:
-                at = slice(kt * TILE, (kt + 1) * TILE)
-                k_ref, v_ref = (pre_keys, pre_values) if kind == "pre" else (keys, values)
-                s = dot(qq, k_ref[p, at, :], ((1,), (1,)))
-                if kind == "diag":
-                    s = jnp.where(causal, s, 0.0)
-                elif kind == "far":
-                    s = jnp.where(causal, 0.0, s)
-                elif kind == "pre":
-                    s = jnp.where(lag <= start + (t * TILE - BAND - kt * TILE), s, 0.0)
-                w = silu_of_half(s).astype(BF16)
-                total = total + dot(w, v_ref[p, at, :], ((1,), (0,)))
-            att[p, t * TILE : (t + 1) * TILE, :] = jnp.where(first_head, total[:TILE], total[TILE:])
+            stack += [jnp.where(first_head, q, zero), jnp.where(first_head, zero, q)]
+        totals = [None] * 4
+        for kind, kt in (("own", 0), ("own", 1), ("own", 2), ("own", 3), ("pre", 0), ("pre", 1)):
+            at = slice(kt * TILE, (kt + 1) * TILE)
+            k_ref, v_ref = (pre_keys, pre_values) if kind == "pre" else (keys, values)
+            here = range(4) if kind == "pre" else range(kt, min(kt + 3, 4))
+            for group in ([here[i : i + 4] for i in range(0, len(here), 4)]):
+                qq = jnp.concatenate(stack[2 * group[0] : 2 * group[-1] + 2], axis=0)
+                s = dot(qq, k_ref[p, :, at], ((1,), (0,)))
+                ws = []
+                for n, t in enumerate(group):
+                    x = s[n * 2 * TILE : (n + 1) * 2 * TILE]
+                    if kind == "pre":
+                        x = jnp.where(lag <= start + (t * TILE - BAND - kt * TILE), x, 0.0)
+                    elif kt == t:
+                        x = jnp.where(causal, x, 0.0)
+                    elif kt == t - 2:
+                        x = jnp.where(causal, 0.0, x)
+                    ws.append(silu_of_half(x).astype(BF16))
+                o = dot(jnp.concatenate(ws, axis=0), v_ref[p, at, :], ((1,), (0,)))
+                for n, t in enumerate(group):
+                    x = o[n * 2 * TILE : (n + 1) * 2 * TILE]
+                    totals[t] = x if totals[t] is None else totals[t] + x
+        for t in range(4):
+            att[p, t * TILE : (t + 1) * TILE, :] = jnp.where(first_head, totals[t][:TILE], totals[t][TILE:])
         return 0
 
-    lax.fori_loop(0, PAIRS, pair, 0)
+    for p in range(PAIRS):
+        pair(p, 0)
 
     for p in range(PAIRS):
         acc_ref[p] = att[p, : 2 * TILE, :]
@@ -250,9 +263,9 @@
         in_specs=[pl.BlockSpec(memory_space=pltpu.SMEM)] + [VM] * (6 + len(buckets)),
         out_specs=[pl.BlockSpec((512, D), lambda i: (1, 0)), VM, VM, VM],
         scratch_shapes=[
+            pltpu.VMEM((PAIRS, PAIR, L), BF16),
             pltpu.VMEM((PAIRS, L, PAIR), BF16),
-            pltpu.VMEM((PAIRS, L, PAIR), BF16),
-            pltpu.VMEM((PAIRS, PREFIX, PAIR), BF16),
+            pltpu.VMEM((PAIRS, PAIR, PREFIX), BF16),
             pltpu.VMEM((PAIRS, PREFIX, PAIR), BF16),
             pltpu.VMEM((PAIRS, L, PAIR), BF16),
             pltpu.VMEM((512, D), BF16),
@@ -274,7 +287,7 @@
         at = slice(t * TILE, (t + 1) * TILE)
         rows = edge_ref[at, :]
         store_pairs(values, at, half_silu_proj(rows, w_ref[:, D : 2 * D]))
-        store_pairs(keys, at, half_silu_proj(rows, w_ref[:, 3 * D :]))
+        store_turned(keys, at, half_silu_proj(rows, w_ref[:, 3 * D :]))
     first_head = head_masks()
     row = lax.broadcasted_iota(jnp.int32, (2 * TILE, TILE), 0)
     a = jnp.where(row < TILE, row, row - TILE)
@@ -289,7 +302,7 @@
             total = jnp.zeros((2 * TILE, PAIR), F32)
             for kt in range(t, 2):
                 at = slice(kt * TILE, (kt + 1) * TILE)
-                s = dot(qq, keys[p, at, :], ((1,), (1,)))
+                s = dot(qq, keys[p, :, at], ((1,), (0,)))
                 if kt == t:
                     s = jnp.where(later, s, 0.0)
                 w = silu_of_half(s).astype(BF16)
@@ -310,7 +323,7 @@
         out_specs=pl.BlockSpec((512, D), lambda i: (0, 0)),
         input_output_aliases={7: 0},
         scratch_shapes=[
-            pltpu.VMEM((PAIRS, BAND, PAIR), BF16),
+            pltpu.VMEM((PAIRS, PAIR, BAND), BF16),
             pltpu.VMEM((PAIRS, BAND, PAIR), BF16),
         ],
         compiler_params=pltpu.CompilerParams(vmem_limit_bytes=VMEM_LIMIT),

time: 90.2 us -> 88.1 us (0.977)
  local copies, waits for them, and re-layouts: 1.24 us -> 0.01 us
    pallas_call x1, Pallas kernels: 17.2 us -> 15.5 us  [main_part(): pl.pallas_call(main_kernel, grid=(1,), out_shape=[jax.ShapeDtypeStruct((L...]
    unnamed x10 -> x8, local copies, waits for them, and re-layouts: 1.24 us -> 0.01 us
    pallas_call x1, Pallas kernels: 3 us -> 3.92 us  [pack(): pl.pallas_call(pack_kernel, grid=(users // part,), out_shape=jax.ShapeDty...]
  transfers between devices with their start and end apart: 9 -> 9, of which waited for: 2 -> 2; matrix products, arithmetic and copies ran while one was open for 0% -> 0% of each run, Pallas kernels for 22% -> 21%
where the time goes in v2:
time: 88.1 us; the launch traced here: 86.9 us
  waiting for transfers between devices  34.8 us (40%)
  Pallas kernels  26.6 us (30%)
  starting transfers between devices  24.6 us (28%)
    ppermute x7, waiting for transfers between devices, local(): lax.ppermute(first, 'ctx', [(0, k)])  24.3 us
    pallas_call x1, Pallas kernels, main_part(): pl.pallas_call(main_kernel, grid=(1,), out_shape=[jax.ShapeDtypeStruct((L...  15.5 us
    all_to_all x1, starting transfers between devices, local(): lax.all_to_all(pack(event_embed, ctx), ('users', 'ctx'), split_axis=0, co...  15.3 us
    all_to_all x1, waiting for transfers between devices, local(): lax.all_to_all(pack(event_embed, ctx), ('users', 'ctx'), split_axis=0, co...  10.5 us
    ppermute x7, starting transfers between devices, local(): lax.ppermute(first, 'ctx', [(0, k)])  5.25 us
    pallas_call x1, Pallas kernels, edge_part(): pl.pallas_call(edge_kernel, grid=(1,), out_shape=jax.ShapeDtypeStruct((L,...  4.5 us
    ppermute x1, starting transfers between devices, local(): edge = lax.ppermute(high, 'ctx', [(i, i + 1) for i in range(ctx - 1)])  4.12 us
    pallas_call x1, Pallas kernels, pack(): pl.pallas_call(pack_kernel, grid=(users // part,), out_shape=jax.ShapeDty...  3.92 us
  transfers between devices with their start and end apart: 9, of which 2 were waited for; matrix products, arithmetic and copies ran while one was open for 0% of the time, Pallas kernels for 21%

profile of v2, /device:TPU:32, one launch (start us, length us, event | category | flops | bytes accessed | tf_op | source)
XLA Modules:
  0.0 86.9 jit_solution(17656903338787288707)
XLA Ops:
  0.0 3.9 %pack.1 = bf16[256,24,128]{2,1,0:T(8,128)(2,1)} custom-call(bf16[2,32,8192]{2,1,0:T(8,128)(2,1)} %x_ref.1), custom_call_target="tpu_custom_call" | custom-call | tf_op jit(solution)/shard_map/pack/pallas_call | solution.py:58
  3.9 0.0 copy-start.2
  3.9 0.0 copy-start.3
  3.9 15.3 %all-to-all-start = ((bf16[256,24,128]{2,1,0:T(8,128)(2,1)}), bf16[256,24,128]{2,1,0:T(8,128)(2,1)}, u32[]{:S(2)}, u32[]{:S(2)}) async-start(bf16[256,24,128]{2,1,0:T(8,128)(2,1)} %pack.1), calls=%async_computation | async-start | bytes 3145728 | tf_op jit(solution)/shard_map/all_to_all | solution.py:340
  19.2 0.0 copy-done.2
  19.2 1.3 %collective-permute-start.1 = (s32[1,512]{1,0:T(1,128)S(1)}, s32[1,512]{1,0:T(1,128)S(1)}, u32[]{:S(2)}, u32[]{:S(2)}) collective-permute-start(s32[1,512]{1,0:T(1,128)S(1)} %get-tuple-element.19), channel_id=1, source_target_pairs={{0,1},{8,9},{16,17},{24,25},{32,33},{40,41},{48,49},{56,57},{64,65... | collective-permute-start | bytes 6152 | tf_op jit(solution)/shard_map/ppermute | solution.py:339
  20.5 0.7 collective-permute-start.2
  21.2 0.7 collective-permute-start.3
  21.9 0.7 collective-permute-start.4
  22.5 0.7 collective-permute-start.5
  23.9 0.1 pad_add_fusion.place_ref
  23.9 0.0 copy-start
  23.9 0.0 copy-start.1
  23.9 24.3 %collective-permute-done.1.refs_1_ = s32[1,512]{1,0:T(1,128)S(1)} collective-permute-done((s32[1,512]{1,0:T(1,128)S(1)}, s32[1,512]{1,0:T(1,128)S(1)}, u32[]{:S(2)}, u32[]{:S(2)}) %collective-permute-start.1) | collective-permute-done | bytes 2080 | tf_op jit(solution)/shard_map/ppermute | solution.py:339
  48.2 0.7 collective-permute-start.6
  48.9 0.0 collective-permute-done.2.refs_2_
  48.9 0.7 collective-permute-start.7
  49.6 10.5 %all-to-all-done.r_ref = bf16[256,24,128]{2,1,0:T(8,128)(2,1)} async-done(((bf16[256,24,128]{2,1,0:T(8,128)(2,1)}), bf16[256,24,128]{2,1,0:T(8,128)(2,1)}, u32[]{:S(2)}, u32[]{:S(2)}) %all-to-all-start) | async-done | bytes 1572896 | tf_op jit(solution)/shard_map/all_to_all | solution.py:340
  60.1 0.0 copy-done.3
  60.1 2.7 %norm.1 = (bf16[512,512]{1,0:T(8,128)(2,1)S(1)}, bf16[512,512]{1,0:T(8,128)(2,1)S(1)}, f32[2048,128]{1,0:T(8,128)S(1)}) custom-call(bf16[256,24,128]{2,1,0:T(8,128)(2,1)} %all-to-all-done.r_ref, s32[1,1024]{1,0:T(1,128)S(1)} %copy-done.2, f32[128,512]{1,0:T(8,128)S(1)} %copy-done.3), custom_call_target="tpu_custom_call" | custom-call | flops 1000000000 | bytes 4000000 | tf_op jit(solution)/shard_map/norm/pallas_call | solution.py:119
  62.7 0.0 collective-permute-done.3.refs_3_
  62.8 4.1 %collective-permute-start = (bf16[512,512]{1,0:T(8,128)(2,1)S(1)}, bf16[512,512]{1,0:T(8,128)(2,1)S(1)}, u32[]{:S(2)}, u32[]{:S(2)}) collective-permute-start(bf16[512,512]{1,0:T(8,128)(2,1)S(1)} %get-tuple-element.12.high_ref), channel_id=1, source_target_pairs={{0,1},{1,2},{2,3},{3,4},{4,5},{5,6},{6,7},{8,9},{9,10},{10,11},{11... | collective-permute-start | bytes 1572872 | tf_op jit(solution)/shard_map/ppermute | solution.py:342
  66.9 0.0 collective-permute-done.4.refs_4_
  66.9 0.0 collective-permute-done.5.refs_5_
  66.9 0.0 collective-permute-done.6.refs_6_
  66.9 0.0 collective-permute-done.7.refs_7_
  66.9 0.0 copy-done
  66.9 0.0 copy-done.1
  66.9 15.5 %main_part.1 = (bf16[1024,512]{1,0:T(8,128)(2,1)}, f32[4,512,128]{2,1,0:T(8,128)S(1)}, bf16[4,512,128]{2,1,0:T(8,128)(2,1)S(1)}, bf16[512,512]{1,0:T(8,128)(2,1)S(1)}) custom-call(s32[2]{0:T(128)S(1)} %pad_add_fusion.place_ref, bf16[512,512]{1,0:T(8,128)(2,1)S(1)} %get-tuple-element.13.low_ref, bf16[512,512]{1,0:T(8,128)(2,1)S(1)} %get-tuple-element.12.high_ref, ...), custom_call_target="tpu_custom_call" | custom-call | flops 20000000000 | bytes 8000000 | tf_op jit(solution)/shard_map/main_part/pallas_call | solution.py:254
  82.4 0.0 collective-permute-done.edge_ref
  82.4 4.5 %edge_part.1 = bf16[1024,512]{1,0:T(8,128)(2,1)} custom-call(s32[2]{0:T(128)S(1)} %pad_add_fusion.place_ref, bf16[512,512]{1,0:T(8,128)(2,1)S(1)} %collective-permute-done.edge_ref, bf16[512,2048]{1,0:T(8,128)(2,1)S(1)} %copy-done, bf16[512,512]{1,0:T(8,128)(2,1)S(1)} %copy-done.1, ...), custom_call_target="tpu_custom_call", output_to_operand_aliasing={{}: (7, {})} | custom-call | tf_op jit(solution)/shard_map/edge_part/pallas_call | solution.py:318
  (1 shorter events, 0.0 us)
Async XLA Ops:
  3.9 15.3 %copy-start.2 = (s32[1,1024]{1,0:T(1,128)S(1)}, s32[1,1024]{1,0:T(1,128)}, u32[]{:S(2)}) copy-start(s32[1,1024]{1,0:T(1,128)} %bucket_ref.1) | copy-start | bytes 12292
  3.9 56.1 %copy-start.3 = (f32[128,512]{1,0:T(8,128)S(1)}, f32[128,512]{1,0:T(8,128)}, u32[]{:S(2)}) copy-start(f32[128,512]{1,0:T(8,128)} %table_ref.3) | copy-start | bytes 786436
  3.9 56.1 %all-to-all-start = ((bf16[256,24,128]{2,1,0:T(8,128)(2,1)}), bf16[256,24,128]{2,1,0:T(8,128)(2,1)}, u32[]{:S(2)}, u32[]{:S(2)}) async-start(bf16[256,24,128]{2,1,0:T(8,128)(2,1)} %pack.1), calls=%async_computation | async-start | bytes 3145728 | tf_op jit(solution)/shard_map/all_to_all | solution.py:340
  19.2 29.0 %collective-permute-start.1 = (s32[1,512]{1,0:T(1,128)S(1)}, s32[1,512]{1,0:T(1,128)S(1)}, u32[]{:S(2)}, u32[]{:S(2)}) collective-permute-start(s32[1,512]{1,0:T(1,128)S(1)} %get-tuple-element.19), channel_id=1, source_target_pairs={{0,1},{8,9},{16,17},{24,25},{32,33},{40,41},{48,49},{56,57},{64,65... | collective-permute-start | bytes 6152 | tf_op jit(solution)/shard_map/ppermute | solution.py:339
  20.5 28.4 %collective-permute-start.2 = (s32[1,512]{1,0:T(1,128)S(1)}, s32[1,512]{1,0:T(1,128)S(1)}, u32[]{:S(2)}, u32[]{:S(2)}) collective-permute-start(s32[1,512]{1,0:T(1,128)S(1)} %get-tuple-element.19), channel_id=1, source_target_pairs={{0,2},{8,10},{16,18},{24,26},{32,34},{40,42},{48,50},{56,58},{64,6... | collective-permute-start | bytes 6152 | tf_op jit(solution)/shard_map/ppermute | solution.py:339
  21.2 41.6 %collective-permute-start.3 = (s32[1,512]{1,0:T(1,128)S(1)}, s32[1,512]{1,0:T(1,128)S(1)}, u32[]{:S(2)}, u32[]{:S(2)}) collective-permute-start(s32[1,512]{1,0:T(1,128)S(1)} %get-tuple-element.19), channel_id=1, source_target_pairs={{0,3},{8,11},{16,19},{24,27},{32,35},{40,43},{48,51},{56,59},{64,6... | collective-permute-start | bytes 6152 | tf_op jit(solution)/shard_map/ppermute | solution.py:339
  21.9 45.0 %collective-permute-start.4 = (s32[1,512]{1,0:T(1,128)S(1)}, s32[1,512]{1,0:T(1,128)S(1)}, u32[]{:S(2)}, u32[]{:S(2)}) collective-permute-start(s32[1,512]{1,0:T(1,128)S(1)} %get-tuple-element.19), channel_id=1, source_target_pairs={{0,4},{8,12},{16,20},{24,28},{32,36},{40,44},{48,52},{56,60},{64,6... | collective-permute-start | bytes 6152 | tf_op jit(solution)/shard_map/ppermute | solution.py:339
  22.5 44.4 %collective-permute-start.5 = (s32[1,512]{1,0:T(1,128)S(1)}, s32[1,512]{1,0:T(1,128)S(1)}, u32[]{:S(2)}, u32[]{:S(2)}) collective-permute-start(s32[1,512]{1,0:T(1,128)S(1)} %get-tuple-element.19), channel_id=1, source_target_pairs={{0,5},{8,13},{16,21},{24,29},{32,37},{40,45},{48,53},{56,61},{64,6... | collective-permute-start | bytes 6152 | tf_op jit(solution)/shard_map/ppermute | solution.py:339
  23.9 43.0 %copy-start = (bf16[512,2048]{1,0:T(8,128)(2,1)S(1)}, bf16[512,2048]{1,0:T(8,128)(2,1)}, u32[]{:S(2)}) copy-start(bf16[512,2048]{1,0:T(8,128)(2,1)} %w_ref.3) | copy-start | bytes 6291460
  23.9 43.0 %copy-start.1 = (bf16[512,512]{1,0:T(8,128)(2,1)S(1)}, bf16[512,512]{1,0:T(8,128)(2,1)}, u32[]{:S(2)}) copy-start(bf16[512,512]{1,0:T(8,128)(2,1)} %w_out_ref.3) | copy-start | bytes 1572868
  48.2 18.7 %collective-permute-start.6 = (s32[1,512]{1,0:T(1,128)S(1)}, s32[1,512]{1,0:T(1,128)S(1)}, u32[]{:S(2)}, u32[]{:S(2)}) collective-permute-start(s32[1,512]{1,0:T(1,128)S(1)} %get-tuple-element.19), channel_id=1, source_target_pairs={{0,6},{8,14},{16,22},{24,30},{32,38},{40,46},{48,54},{56,62},{64,7... | collective-permute-start | bytes 6152 | tf_op jit(solution)/shard_map/ppermute | solution.py:339
  48.9 18.0 %collective-permute-start.7 = (s32[1,512]{1,0:T(1,128)S(1)}, s32[1,512]{1,0:T(1,128)S(1)}, u32[]{:S(2)}, u32[]{:S(2)}) collective-permute-start(s32[1,512]{1,0:T(1,128)S(1)} %get-tuple-element.19), channel_id=1, source_target_pairs={{0,7},{8,15},{16,23},{24,31},{32,39},{40,47},{48,55},{56,63},{64,7... | collective-permute-start | bytes 6152 | tf_op jit(solution)/shard_map/ppermute | solution.py:339
  62.8 19.7 %collective-permute-start = (bf16[512,512]{1,0:T(8,128)(2,1)S(1)}, bf16[512,512]{1,0:T(8,128)(2,1)S(1)}, u32[]{:S(2)}, u32[]{:S(2)}) collective-permute-start(bf16[512,512]{1,0:T(8,128)(2,1)S(1)} %get-tuple-element.12.high_ref), channel_id=1, source_target_pairs={{0,1},{1,2},{2,3},{3,4},{4,5},{5,6},{6,7},{8,9},{9,10},{10,11},{11... | collective-permute-start | bytes 1572872 | tf_op jit(solution)/shard_map/ppermute | solution.py:342

commit v3 on v2

--- a/solution.py
+++ b/solution.py
@@ -34,22 +34,23 @@
     users = x_ref.shape[1]
     blocks = x_ref.shape[2] // BLK
     ctx = out_ref.shape[0] // users
+    pitch = rows.shape[0] // (2 * users)
     for k in range(2):
         for t in range(blocks):
             part = x_ref[k, :, t * BLK : (t + 1) * BLK].astype(F32)
-            rows[pl.ds(k * users * blocks + t, users, stride=blocks), :] = part
+            rows[pl.ds(k * users * pitch + t, users, stride=pitch), :] = part
             if t < 4:
                 head_rows[pl.ds(k * 4 + t, users, stride=8), :] = part
 
     def user(u, _):
         head = head_rows[pl.ds(pl.multiple_of(u * 8, 8), 8), :]
         for c in range(ctx):
-            first = rows[pl.ds(pl.multiple_of(u * blocks + c * 8, 8), 8), :]
-            second = rows[pl.ds(pl.multiple_of((users + u) * blocks + c * 8, 8), 8), :]
+            first = rows[pl.ds(pl.multiple_of(u * pitch + c * 8, 8), 8), :]
+            second = rows[pl.ds(pl.multiple_of((users + u) * pitch + c * 8, 8), 8), :]
             out_ref[u * ctx + c] = jnp.concatenate([first, second, head], axis=0).astype(BF16)
         return 0
 
-    lax.fori_loop(0, users, user, 0, unroll=2)
+    lax.fori_loop(0, users, user, 0, unroll=8)
 
 
 def pack(x, ctx):
@@ -62,7 +63,7 @@
         in_specs=[pl.BlockSpec((2, part, events), lambda i: (0, i, 0))],
         out_specs=pl.BlockSpec((part * ctx, 24, BLK), lambda i: (i, 0, 0)),
         scratch_shapes=[
-            pltpu.VMEM((2 * part * events // BLK, BLK), F32),
+            pltpu.VMEM((2 * part * (events // BLK + 8), BLK), F32),
             pltpu.VMEM((part * 8, BLK), F32),
         ],
         compiler_params=pltpu.CompilerParams(vmem_limit_bytes=PACK_LIMIT),
@@ -107,7 +108,7 @@
             pre_ref[pl.ds(pl.multiple_of(s * 8, 128), 128), :] = part[:, 16:].reshape(128, BLK)
             return 0
 
-        lax.fori_loop(0, step // 16, widen, 0)
+        lax.fori_loop(0, step // 16, widen, 0, unroll=4)
     for j in (4, 5, 6, 7, 0, 1, 2, 3):
         hot = slot == bucket_ref[:, j * BLK : (j + 1) * BLK]
         out_ref = low_ref if j < 4 else high_ref

time: 88.1 us -> 86.6 us (0.983)
  Pallas kernels: 26.6 us -> 25 us
    pallas_call x1, Pallas kernels: 3.92 us -> 2.42 us  [pack(): pl.pallas_call(pack_kernel, grid=(users // part,), out_shape=jax.ShapeDty...]
where the time goes in v3:
time: 86.6 us; the launch traced here: 85.4 us
  waiting for transfers between devices  34.8 us (40%)
  Pallas kernels  25 us (29%)
  starting transfers between devices  24.6 us (28%)
    ppermute x7, waiting for transfers between devices, local(): lax.ppermute(first, 'ctx', [(0, k)])  24.3 us
    pallas_call x1, Pallas kernels, main_part(): pl.pallas_call(main_kernel, grid=(1,), out_shape=[jax.ShapeDtypeStruct((L...  15.5 us
    all_to_all x1, starting transfers between devices, local(): lax.all_to_all(pack(event_embed, ctx), ('users', 'ctx'), split_axis=0, co...  15.3 us
    all_to_all x1, waiting for transfers between devices, local(): lax.all_to_all(pack(event_embed, ctx), ('users', 'ctx'), split_axis=0, co...  10.5 us
    ppermute x7, starting transfers between devices, local(): lax.ppermute(first, 'ctx', [(0, k)])  5.25 us
    pallas_call x1, Pallas kernels, edge_part(): pl.pallas_call(edge_kernel, grid=(1,), out_shape=jax.ShapeDtypeStruct((L,...  4.5 us
    ppermute x1, starting transfers between devices, local(): edge = lax.ppermute(high, 'ctx', [(i, i + 1) for i in range(ctx - 1)])  4.12 us
    pallas_call x1, Pallas kernels, norm(): pl.pallas_call(norm_kernel, out_shape=[half, half, jax.ShapeDtypeStruct((...  2.61 us
  transfers between devices with their start and end apart: 9, of which 2 were waited for; matrix products, arithmetic and copies ran while one was open for 0% of the time, Pallas kernels for 21%

profile of v3, /device:TPU:32, one launch (start us, length us, event | category | flops | bytes accessed | tf_op | source)
XLA Modules:
  0.0 85.4 jit_solution(14984827436921038907)
XLA Ops:
  0.0 2.4 %pack.1 = bf16[256,24,128]{2,1,0:T(8,128)(2,1)} custom-call(bf16[2,32,8192]{2,1,0:T(8,128)(2,1)} %x_ref.1), custom_call_target="tpu_custom_call" | custom-call | tf_op jit(solution)/shard_map/pack/pallas_call | solution.py:59
  2.4 0.0 copy-start.2
  2.4 0.0 copy-start.3
  2.4 15.3 %all-to-all-start = ((bf16[256,24,128]{2,1,0:T(8,128)(2,1)}), bf16[256,24,128]{2,1,0:T(8,128)(2,1)}, u32[]{:S(2)}, u32[]{:S(2)}) async-start(bf16[256,24,128]{2,1,0:T(8,128)(2,1)} %pack.1), calls=%async_computation | async-start | bytes 3145728 | tf_op jit(solution)/shard_map/all_to_all | solution.py:341
  17.7 0.0 copy-done.2
  17.7 1.3 %collective-permute-start.1 = (s32[1,512]{1,0:T(1,128)S(1)}, s32[1,512]{1,0:T(1,128)S(1)}, u32[]{:S(2)}, u32[]{:S(2)}) collective-permute-start(s32[1,512]{1,0:T(1,128)S(1)} %get-tuple-element.19), channel_id=1, source_target_pairs={{0,1},{8,9},{16,17},{24,25},{32,33},{40,41},{48,49},{56,57},{64,65... | collective-permute-start | bytes 6152 | tf_op jit(solution)/shard_map/ppermute | solution.py:340
  19.0 0.7 collective-permute-start.2
  19.7 0.7 collective-permute-start.3
  20.4 0.7 collective-permute-start.4
  21.0 0.7 collective-permute-start.5
  22.3 0.1 pad_add_fusion.place_ref
  22.4 0.0 copy-start
  22.4 0.0 copy-start.1
  22.4 24.3 %collective-permute-done.1.refs_1_ = s32[1,512]{1,0:T(1,128)S(1)} collective-permute-done((s32[1,512]{1,0:T(1,128)S(1)}, s32[1,512]{1,0:T(1,128)S(1)}, u32[]{:S(2)}, u32[]{:S(2)}) %collective-permute-start.1) | collective-permute-done | bytes 2080 | tf_op jit(solution)/shard_map/ppermute | solution.py:340
  46.7 0.7 collective-permute-start.6
  47.4 0.0 collective-permute-done.2.refs_2_
  47.4 0.7 collective-permute-start.7
  48.1 10.5 %all-to-all-done.r_ref = bf16[256,24,128]{2,1,0:T(8,128)(2,1)} async-done(((bf16[256,24,128]{2,1,0:T(8,128)(2,1)}), bf16[256,24,128]{2,1,0:T(8,128)(2,1)}, u32[]{:S(2)}, u32[]{:S(2)}) %all-to-all-start) | async-done | bytes 1572896 | tf_op jit(solution)/shard_map/all_to_all | solution.py:341
  58.6 0.0 copy-done.3
  58.6 2.6 %norm.1 = (bf16[512,512]{1,0:T(8,128)(2,1)S(1)}, bf16[512,512]{1,0:T(8,128)(2,1)S(1)}, f32[2048,128]{1,0:T(8,128)S(1)}) custom-call(bf16[256,24,128]{2,1,0:T(8,128)(2,1)} %all-to-all-done.r_ref, s32[1,1024]{1,0:T(1,128)S(1)} %copy-done.2, f32[128,512]{1,0:T(8,128)S(1)} %copy-done.3), custom_call_target="tpu_custom_call" | custom-call | flops 1000000000 | bytes 4000000 | tf_op jit(solution)/shard_map/norm/pallas_call | solution.py:120
  61.2 0.0 collective-permute-done.3.refs_3_
  61.2 4.1 %collective-permute-start = (bf16[512,512]{1,0:T(8,128)(2,1)S(1)}, bf16[512,512]{1,0:T(8,128)(2,1)S(1)}, u32[]{:S(2)}, u32[]{:S(2)}) collective-permute-start(bf16[512,512]{1,0:T(8,128)(2,1)S(1)} %get-tuple-element.12.high_ref), channel_id=1, source_target_pairs={{0,1},{1,2},{2,3},{3,4},{4,5},{5,6},{6,7},{8,9},{9,10},{10,11},{11... | collective-permute-start | bytes 1572872 | tf_op jit(solution)/shard_map/ppermute | solution.py:343
  65.3 0.0 collective-permute-done.4.refs_4_
  65.3 0.0 collective-permute-done.5.refs_5_
  65.3 0.0 collective-permute-done.6.refs_6_
  65.4 0.0 collective-permute-done.7.refs_7_
  65.4 0.0 copy-done
  65.4 0.0 copy-done.1
  65.4 15.5 %main_part.1 = (bf16[1024,512]{1,0:T(8,128)(2,1)}, f32[4,512,128]{2,1,0:T(8,128)S(1)}, bf16[4,512,128]{2,1,0:T(8,128)(2,1)S(1)}, bf16[512,512]{1,0:T(8,128)(2,1)S(1)}) custom-call(s32[2]{0:T(128)S(1)} %pad_add_fusion.place_ref, bf16[512,512]{1,0:T(8,128)(2,1)S(1)} %get-tuple-element.13.low_ref, bf16[512,512]{1,0:T(8,128)(2,1)S(1)} %get-tuple-element.12.high_ref, ...), custom_call_target="tpu_custom_call" | custom-call | flops 20000000000 | bytes 8000000 | tf_op jit(solution)/shard_map/main_part/pallas_call | solution.py:255
  80.9 0.0 collective-permute-done.edge_ref
  80.9 4.5 %edge_part.1 = bf16[1024,512]{1,0:T(8,128)(2,1)} custom-call(s32[2]{0:T(128)S(1)} %pad_add_fusion.place_ref, bf16[512,512]{1,0:T(8,128)(2,1)S(1)} %collective-permute-done.edge_ref, bf16[512,2048]{1,0:T(8,128)(2,1)S(1)} %copy-done, bf16[512,512]{1,0:T(8,128)(2,1)S(1)} %copy-done.1, ...), custom_call_target="tpu_custom_call", output_to_operand_aliasing={{}: (7, {})} | custom-call | tf_op jit(solution)/shard_map/edge_part/pallas_call | solution.py:319
  (1 shorter events, 0.0 us)
Async XLA Ops:
  2.4 15.3 %copy-start.2 = (s32[1,1024]{1,0:T(1,128)S(1)}, s32[1,1024]{1,0:T(1,128)}, u32[]{:S(2)}) copy-start(s32[1,1024]{1,0:T(1,128)} %bucket_ref.1) | copy-start | bytes 12292
  2.4 56.1 %copy-start.3 = (f32[128,512]{1,0:T(8,128)S(1)}, f32[128,512]{1,0:T(8,128)}, u32[]{:S(2)}) copy-start(f32[128,512]{1,0:T(8,128)} %table_ref.3) | copy-start | bytes 786436
  2.4 56.1 %all-to-all-start = ((bf16[256,24,128]{2,1,0:T(8,128)(2,1)}), bf16[256,24,128]{2,1,0:T(8,128)(2,1)}, u32[]{:S(2)}, u32[]{:S(2)}) async-start(bf16[256,24,128]{2,1,0:T(8,128)(2,1)} %pack.1), calls=%async_computation | async-start | bytes 3145728 | tf_op jit(solution)/shard_map/all_to_all | solution.py:341
  17.7 29.0 %collective-permute-start.1 = (s32[1,512]{1,0:T(1,128)S(1)}, s32[1,512]{1,0:T(1,128)S(1)}, u32[]{:S(2)}, u32[]{:S(2)}) collective-permute-start(s32[1,512]{1,0:T(1,128)S(1)} %get-tuple-element.19), channel_id=1, source_target_pairs={{0,1},{8,9},{16,17},{24,25},{32,33},{40,41},{48,49},{56,57},{64,65... | collective-permute-start | bytes 6152 | tf_op jit(solution)/shard_map/ppermute | solution.py:340
  19.0 28.4 %collective-permute-start.2 = (s32[1,512]{1,0:T(1,128)S(1)}, s32[1,512]{1,0:T(1,128)S(1)}, u32[]{:S(2)}, u32[]{:S(2)}) collective-permute-start(s32[1,512]{1,0:T(1,128)S(1)} %get-tuple-element.19), channel_id=1, source_target_pairs={{0,2},{8,10},{16,18},{24,26},{32,34},{40,42},{48,50},{56,58},{64,6... | collective-permute-start | bytes 6152 | tf_op jit(solution)/shard_map/ppermute | solution.py:340
  19.7 41.5 %collective-permute-start.3 = (s32[1,512]{1,0:T(1,128)S(1)}, s32[1,512]{1,0:T(1,128)S(1)}, u32[]{:S(2)}, u32[]{:S(2)}) collective-permute-start(s32[1,512]{1,0:T(1,128)S(1)} %get-tuple-element.19), channel_id=1, source_target_pairs={{0,3},{8,11},{16,19},{24,27},{32,35},{40,43},{48,51},{56,59},{64,6... | collective-permute-start | bytes 6152 | tf_op jit(solution)/shard_map/ppermute | solution.py:340
  20.4 45.0 %collective-permute-start.4 = (s32[1,512]{1,0:T(1,128)S(1)}, s32[1,512]{1,0:T(1,128)S(1)}, u32[]{:S(2)}, u32[]{:S(2)}) collective-permute-start(s32[1,512]{1,0:T(1,128)S(1)} %get-tuple-element.19), channel_id=1, source_target_pairs={{0,4},{8,12},{16,20},{24,28},{32,36},{40,44},{48,52},{56,60},{64,6... | collective-permute-start | bytes 6152 | tf_op jit(solution)/shard_map/ppermute | solution.py:340
  21.0 44.3 %collective-permute-start.5 = (s32[1,512]{1,0:T(1,128)S(1)}, s32[1,512]{1,0:T(1,128)S(1)}, u32[]{:S(2)}, u32[]{:S(2)}) collective-permute-start(s32[1,512]{1,0:T(1,128)S(1)} %get-tuple-element.19), channel_id=1, source_target_pairs={{0,5},{8,13},{16,21},{24,29},{32,37},{40,45},{48,53},{56,61},{64,6... | collective-permute-start | bytes 6152 | tf_op jit(solution)/shard_map/ppermute | solution.py:340
  22.4 42.9 %copy-start = (bf16[512,2048]{1,0:T(8,128)(2,1)S(1)}, bf16[512,2048]{1,0:T(8,128)(2,1)}, u32[]{:S(2)}) copy-start(bf16[512,2048]{1,0:T(8,128)(2,1)} %w_ref.3) | copy-start | bytes 6291460
  22.4 43.0 %copy-start.1 = (bf16[512,512]{1,0:T(8,128)(2,1)S(1)}, bf16[512,512]{1,0:T(8,128)(2,1)}, u32[]{:S(2)}) copy-start(bf16[512,512]{1,0:T(8,128)(2,1)} %w_out_ref.3) | copy-start | bytes 1572868
  46.7 18.6 %collective-permute-start.6 = (s32[1,512]{1,0:T(1,128)S(1)}, s32[1,512]{1,0:T(1,128)S(1)}, u32[]{:S(2)}, u32[]{:S(2)}) collective-permute-start(s32[1,512]{1,0:T(1,128)S(1)} %get-tuple-element.19), channel_id=1, source_target_pairs={{0,6},{8,14},{16,22},{24,30},{32,38},{40,46},{48,54},{56,62},{64,7... | collective-permute-start | bytes 6152 | tf_op jit(solution)/shard_map/ppermute | solution.py:340
  47.4 18.0 %collective-permute-start.7 = (s32[1,512]{1,0:T(1,128)S(1)}, s32[1,512]{1,0:T(1,128)S(1)}, u32[]{:S(2)}, u32[]{:S(2)}) collective-permute-start(s32[1,512]{1,0:T(1,128)S(1)} %get-tuple-element.19), channel_id=1, source_target_pairs={{0,7},{8,15},{16,23},{24,31},{32,39},{40,47},{48,55},{56,63},{64,7... | collective-permute-start | bytes 6152 | tf_op jit(solution)/shard_map/ppermute | solution.py:340
  61.2 19.7 %collective-permute-start = (bf16[512,512]{1,0:T(8,128)(2,1)S(1)}, bf16[512,512]{1,0:T(8,128)(2,1)S(1)}, u32[]{:S(2)}, u32[]{:S(2)}) collective-permute-start(bf16[512,512]{1,0:T(8,128)(2,1)S(1)} %get-tuple-element.12.high_ref), channel_id=1, source_target_pairs={{0,1},{1,2},{2,3},{3,4},{4,5},{5,6},{6,7},{8,9},{9,10},{10,11},{11... | collective-permute-start | bytes 1572872 | tf_op jit(solution)/shard_map/ppermute | solution.py:343

commit v4 on v3

--- a/solution.py
+++ b/solution.py
@@ -235,14 +235,17 @@
                     x = o[n * 2 * TILE : (n + 1) * 2 * TILE]
                     totals[t] = x if totals[t] is None else totals[t] + x
         for t in range(4):
-            att[p, t * TILE : (t + 1) * TILE, :] = jnp.where(first_head, totals[t][:TILE], totals[t][TILE:])
+            part = jnp.where(first_head, totals[t][:TILE], totals[t][TILE:])
+            if t < 2:
+                acc_ref[p, t * TILE : (t + 1) * TILE, :] = part
+            else:
+                att[p, t * TILE : (t + 1) * TILE, :] = part
         return 0
 
     for p in range(PAIRS):
         pair(p, 0)
 
     for p in range(PAIRS):
-        acc_ref[p] = att[p, : 2 * TILE, :]
         query_ref[p] = queries[p, : 2 * TILE, :]
     for t in (2, 3):
         whole = jnp.concatenate([att[p, t * TILE : (t + 1) * TILE, :] for p in range(PAIRS)], axis=1)
@@ -280,7 +283,7 @@
 
 def edge_kernel(
     place_ref, edge_ref, w_ref, w_out_ref, acc_ref, query_ref, gate_ref, prev_ref,
-    out_ref, keys, values,
+    out_hbm, keys, values, out_ref, sem,
 ):
     start = place_ref[0] * L
     length = place_ref[1]
@@ -293,6 +296,7 @@
     row = lax.broadcasted_iota(jnp.int32, (2 * TILE, TILE), 0)
     a = jnp.where(row < TILE, row, row - TILE)
     later = lax.broadcasted_iota(jnp.int32, (2 * TILE, TILE), 1) > a
+    copies = []
     for t in range(2):
         here = slice(t * TILE, (t + 1) * TILE)
         columns = []
@@ -313,19 +317,24 @@
         out_ref[here, :] = finish(
             whole, gate_ref[here, :], row_scale(start + t * TILE, length), w_out_ref[...]
         )
+        copies.append(pltpu.make_async_copy(out_ref.at[here], out_hbm.at[here], sem.at[t]))
+        copies[t].start()
+    for copy in copies:
+        copy.wait()
 
 
 def edge_part(place, edge, w, w_out, acc, query, gate, prev):
     return pl.pallas_call(
         edge_kernel,
-        grid=(1,),
         out_shape=jax.ShapeDtypeStruct((L, D), BF16),
         in_specs=[pl.BlockSpec(memory_space=pltpu.SMEM)] + [VM] * 6 + [pl.BlockSpec(memory_space=pl.ANY)],
-        out_specs=pl.BlockSpec((512, D), lambda i: (0, 0)),
+        out_specs=pl.BlockSpec(memory_space=pl.ANY),
         input_output_aliases={7: 0},
         scratch_shapes=[
             pltpu.VMEM((PAIRS, PAIR, BAND), BF16),
             pltpu.VMEM((PAIRS, BAND, PAIR), BF16),
+            pltpu.VMEM((2 * TILE, D), BF16),
+            pltpu.SemaphoreType.DMA((2,)),
         ],
         compiler_params=pltpu.CompilerParams(vmem_limit_bytes=VMEM_LIMIT),
         name="edge_part",

time: 86.6 us -> 86.7 us (level)
  no operation moved by 1% of the time
where the time goes in v4:
time: 86.7 us; the launch traced here: 85.5 us
  waiting for transfers between devices  34.8 us (40%)
  Pallas kernels  25 us (29%)
  starting transfers between devices  24.6 us (28%)
  between operations  1 us (1%)
    ppermute x7, waiting for transfers between devices, local(): lax.ppermute(first, 'ctx', [(0, k)])  24.3 us
    pallas_call x1, Pallas kernels, main_part(): pl.pallas_call(main_kernel, grid=(1,), out_shape=[jax.ShapeDtypeStruct((L...  15.5 us
    all_to_all x1, starting transfers between devices, local(): lax.all_to_all(pack(event_embed, ctx), ('users', 'ctx'), split_axis=0, co...  15.3 us
    all_to_all x1, waiting for transfers between devices, local(): lax.all_to_all(pack(event_embed, ctx), ('users', 'ctx'), split_axis=0, co...  10.5 us
    ppermute x7, starting transfers between devices, local(): lax.ppermute(first, 'ctx', [(0, k)])  5.25 us
    pallas_call x1, Pallas kernels, edge_part(): pl.pallas_call(edge_kernel, out_shape=jax.ShapeDtypeStruct((L, D), BF16),...  4.43 us
    ppermute x1, starting transfers between devices, local(): edge = lax.ppermute(high, 'ctx', [(i, i + 1) for i in range(ctx - 1)])  4.12 us
    pallas_call x1, Pallas kernels, norm(): pl.pallas_call(norm_kernel, out_shape=[half, half, jax.ShapeDtypeStruct((...  2.61 us
  transfers between devices with their start and end apart: 9, of which 2 were waited for; matrix products, arithmetic and copies ran while one was open for 0% of the time, Pallas kernels for 21%

profile of v4, /device:TPU:32, one launch (start us, length us, event | category | flops | bytes accessed | tf_op | source)
XLA Modules:
  0.0 85.5 jit_solution(17073329675673346565)
XLA Ops:
  0.0 2.4 %pack.1 = bf16[256,24,128]{2,1,0:T(8,128)(2,1)} custom-call(bf16[2,32,8192]{2,1,0:T(8,128)(2,1)} %x_ref.1), custom_call_target="tpu_custom_call" | custom-call | tf_op jit(solution)/shard_map/pack/pallas_call | solution.py:59
  2.4 0.0 copy-start.2
  2.4 0.0 copy-start.3
  2.4 15.3 %all-to-all-start = ((bf16[256,24,128]{2,1,0:T(8,128)(2,1)}), bf16[256,24,128]{2,1,0:T(8,128)(2,1)}, u32[]{:S(2)}, u32[]{:S(2)}) async-start(bf16[256,24,128]{2,1,0:T(8,128)(2,1)} %pack.1), calls=%async_computation | async-start | bytes 3145728 | tf_op jit(solution)/shard_map/all_to_all | solution.py:350
  17.7 0.0 copy-done.2
  17.7 1.3 %collective-permute-start.1 = (s32[1,512]{1,0:T(1,128)S(1)}, s32[1,512]{1,0:T(1,128)S(1)}, u32[]{:S(2)}, u32[]{:S(2)}) collective-permute-start(s32[1,512]{1,0:T(1,128)S(1)} %get-tuple-element.19), channel_id=1, source_target_pairs={{0,1},{8,9},{16,17},{24,25},{32,33},{40,41},{48,49},{56,57},{64,65... | collective-permute-start | bytes 6152 | tf_op jit(solution)/shard_map/ppermute | solution.py:349
  19.0 0.7 collective-permute-start.2
  19.7 0.7 collective-permute-start.3
  20.4 0.7 collective-permute-start.4
  21.0 0.7 collective-permute-start.5
  22.3 0.1 pad_add_fusion.place_ref
  22.4 0.0 copy-start
  22.4 0.0 copy-start.1
  22.4 24.3 %collective-permute-done.1.refs_1_ = s32[1,512]{1,0:T(1,128)S(1)} collective-permute-done((s32[1,512]{1,0:T(1,128)S(1)}, s32[1,512]{1,0:T(1,128)S(1)}, u32[]{:S(2)}, u32[]{:S(2)}) %collective-permute-start.1) | collective-permute-done | bytes 2080 | tf_op jit(solution)/shard_map/ppermute | solution.py:349
  46.7 0.7 collective-permute-start.6
  47.4 0.0 collective-permute-done.2.refs_2_
  47.4 0.7 collective-permute-start.7
  48.1 10.5 %all-to-all-done.r_ref = bf16[256,24,128]{2,1,0:T(8,128)(2,1)} async-done(((bf16[256,24,128]{2,1,0:T(8,128)(2,1)}), bf16[256,24,128]{2,1,0:T(8,128)(2,1)}, u32[]{:S(2)}, u32[]{:S(2)}) %all-to-all-start) | async-done | bytes 1572896 | tf_op jit(solution)/shard_map/all_to_all | solution.py:350
  58.6 0.0 copy-done.3
  58.6 2.6 %norm.1 = (bf16[512,512]{1,0:T(8,128)(2,1)S(1)}, bf16[512,512]{1,0:T(8,128)(2,1)S(1)}, f32[2048,128]{1,0:T(8,128)S(1)}) custom-call(bf16[256,24,128]{2,1,0:T(8,128)(2,1)} %all-to-all-done.r_ref, s32[1,1024]{1,0:T(1,128)S(1)} %copy-done.2, f32[128,512]{1,0:T(8,128)S(1)} %copy-done.3), custom_call_target="tpu_custom_call" | custom-call | flops 1000000000 | bytes 4000000 | tf_op jit(solution)/shard_map/norm/pallas_call | solution.py:120
  61.2 0.0 collective-permute-done.3.refs_3_
  61.2 4.1 %collective-permute-start = (bf16[512,512]{1,0:T(8,128)(2,1)S(1)}, bf16[512,512]{1,0:T(8,128)(2,1)S(1)}, u32[]{:S(2)}, u32[]{:S(2)}) collective-permute-start(bf16[512,512]{1,0:T(8,128)(2,1)S(1)} %get-tuple-element.12.high_ref), channel_id=1, source_target_pairs={{0,1},{1,2},{2,3},{3,4},{4,5},{5,6},{6,7},{8,9},{9,10},{10,11},{11... | collective-permute-start | bytes 1572872 | tf_op jit(solution)/shard_map/ppermute | solution.py:352
  65.3 0.0 collective-permute-done.4.refs_4_
  65.3 0.0 collective-permute-done.5.refs_5_
  65.3 0.0 collective-permute-done.6.refs_6_
  65.4 0.0 collective-permute-done.7.refs_7_
  65.4 0.0 copy-done
  65.4 0.0 copy-done.1
  65.4 15.5 %main_part.1 = (bf16[1024,512]{1,0:T(8,128)(2,1)}, f32[4,512,128]{2,1,0:T(8,128)S(1)}, bf16[4,512,128]{2,1,0:T(8,128)(2,1)S(1)}, bf16[512,512]{1,0:T(8,128)(2,1)S(1)}) custom-call(s32[2]{0:T(128)S(1)} %pad_add_fusion.place_ref, bf16[512,512]{1,0:T(8,128)(2,1)S(1)} %get-tuple-element.13.low_ref, bf16[512,512]{1,0:T(8,128)(2,1)S(1)} %get-tuple-element.12.high_ref, ...), custom_call_target="tpu_custom_call" | custom-call | flops 20000000000 | bytes 8000000 | tf_op jit(solution)/shard_map/main_part/pallas_call | solution.py:258
  80.9 0.0 collective-permute-done.edge_ref
  80.9 4.4 %edge_part.1 = bf16[1024,512]{1,0:T(8,128)(2,1)} custom-call(s32[2]{0:T(128)S(1)} %pad_add_fusion.place_ref, bf16[512,512]{1,0:T(8,128)(2,1)S(1)} %collective-permute-done.edge_ref, bf16[512,2048]{1,0:T(8,128)(2,1)S(1)} %copy-done, bf16[512,512]{1,0:T(8,128)(2,1)S(1)} %copy-done.1, ...), custom_call_target="tpu_custom_call", output_to_operand_aliasing={{}: (7, {})} | custom-call | tf_op jit(solution)/shard_map/edge_part/pallas_call | solution.py:327
  (1 shorter events, 0.0 us)
Async XLA Ops:
  2.4 15.3 %copy-start.2 = (s32[1,1024]{1,0:T(1,128)S(1)}, s32[1,1024]{1,0:T(1,128)}, u32[]{:S(2)}) copy-start(s32[1,1024]{1,0:T(1,128)} %bucket_ref.1) | copy-start | bytes 12292
  2.4 56.1 %copy-start.3 = (f32[128,512]{1,0:T(8,128)S(1)}, f32[128,512]{1,0:T(8,128)}, u32[]{:S(2)}) copy-start(f32[128,512]{1,0:T(8,128)} %table_ref.3) | copy-start | bytes 786436
  2.4 56.1 %all-to-all-start = ((bf16[256,24,128]{2,1,0:T(8,128)(2,1)}), bf16[256,24,128]{2,1,0:T(8,128)(2,1)}, u32[]{:S(2)}, u32[]{:S(2)}) async-start(bf16[256,24,128]{2,1,0:T(8,128)(2,1)} %pack.1), calls=%async_computation | async-start | bytes 3145728 | tf_op jit(solution)/shard_map/all_to_all | solution.py:350
  17.7 29.0 %collective-permute-start.1 = (s32[1,512]{1,0:T(1,128)S(1)}, s32[1,512]{1,0:T(1,128)S(1)}, u32[]{:S(2)}, u32[]{:S(2)}) collective-permute-start(s32[1,512]{1,0:T(1,128)S(1)} %get-tuple-element.19), channel_id=1, source_target_pairs={{0,1},{8,9},{16,17},{24,25},{32,33},{40,41},{48,49},{56,57},{64,65... | collective-permute-start | bytes 6152 | tf_op jit(solution)/shard_map/ppermute | solution.py:349
  19.0 28.4 %collective-permute-start.2 = (s32[1,512]{1,0:T(1,128)S(1)}, s32[1,512]{1,0:T(1,128)S(1)}, u32[]{:S(2)}, u32[]{:S(2)}) collective-permute-start(s32[1,512]{1,0:T(1,128)S(1)} %get-tuple-element.19), channel_id=1, source_target_pairs={{0,2},{8,10},{16,18},{24,26},{32,34},{40,42},{48,50},{56,58},{64,6... | collective-permute-start | bytes 6152 | tf_op jit(solution)/shard_map/ppermute | solution.py:349
  19.7 41.5 %collective-permute-start.3 = (s32[1,512]{1,0:T(1,128)S(1)}, s32[1,512]{1,0:T(1,128)S(1)}, u32[]{:S(2)}, u32[]{:S(2)}) collective-permute-start(s32[1,512]{1,0:T(1,128)S(1)} %get-tuple-element.19), channel_id=1, source_target_pairs={{0,3},{8,11},{16,19},{24,27},{32,35},{40,43},{48,51},{56,59},{64,6... | collective-permute-start | bytes 6152 | tf_op jit(solution)/shard_map/ppermute | solution.py:349
  20.4 45.0 %collective-permute-start.4 = (s32[1,512]{1,0:T(1,128)S(1)}, s32[1,512]{1,0:T(1,128)S(1)}, u32[]{:S(2)}, u32[]{:S(2)}) collective-permute-start(s32[1,512]{1,0:T(1,128)S(1)} %get-tuple-element.19), channel_id=1, source_target_pairs={{0,4},{8,12},{16,20},{24,28},{32,36},{40,44},{48,52},{56,60},{64,6... | collective-permute-start | bytes 6152 | tf_op jit(solution)/shard_map/ppermute | solution.py:349
  21.0 44.3 %collective-permute-start.5 = (s32[1,512]{1,0:T(1,128)S(1)}, s32[1,512]{1,0:T(1,128)S(1)}, u32[]{:S(2)}, u32[]{:S(2)}) collective-permute-start(s32[1,512]{1,0:T(1,128)S(1)} %get-tuple-element.19), channel_id=1, source_target_pairs={{0,5},{8,13},{16,21},{24,29},{32,37},{40,45},{48,53},{56,61},{64,6... | collective-permute-start | bytes 6152 | tf_op jit(solution)/shard_map/ppermute | solution.py:349
  22.4 42.9 %copy-start = (bf16[512,2048]{1,0:T(8,128)(2,1)S(1)}, bf16[512,2048]{1,0:T(8,128)(2,1)}, u32[]{:S(2)}) copy-start(bf16[512,2048]{1,0:T(8,128)(2,1)} %w_ref.3) | copy-start | bytes 6291460
  22.4 43.0 %copy-start.1 = (bf16[512,512]{1,0:T(8,128)(2,1)S(1)}, bf16[512,512]{1,0:T(8,128)(2,1)}, u32[]{:S(2)}) copy-start(bf16[512,512]{1,0:T(8,128)(2,1)} %w_out_ref.3) | copy-start | bytes 1572868
  46.7 18.6 %collective-permute-start.6 = (s32[1,512]{1,0:T(1,128)S(1)}, s32[1,512]{1,0:T(1,128)S(1)}, u32[]{:S(2)}, u32[]{:S(2)}) collective-permute-start(s32[1,512]{1,0:T(1,128)S(1)} %get-tuple-element.19), channel_id=1, source_target_pairs={{0,6},{8,14},{16,22},{24,30},{32,38},{40,46},{48,54},{56,62},{64,7... | collective-permute-start | bytes 6152 | tf_op jit(solution)/shard_map/ppermute | solution.py:349
  47.4 18.0 %collective-permute-start.7 = (s32[1,512]{1,0:T(1,128)S(1)}, s32[1,512]{1,0:T(1,128)S(1)}, u32[]{:S(2)}, u32[]{:S(2)}) collective-permute-start(s32[1,512]{1,0:T(1,128)S(1)} %get-tuple-element.19), channel_id=1, source_target_pairs={{0,7},{8,15},{16,23},{24,31},{32,39},{40,47},{48,55},{56,63},{64,7... | collective-permute-start | bytes 6152 | tf_op jit(solution)/shard_map/ppermute | solution.py:349
  61.2 19.7 %collective-permute-start = (bf16[512,512]{1,0:T(8,128)(2,1)S(1)}, bf16[512,512]{1,0:T(8,128)(2,1)S(1)}, u32[]{:S(2)}, u32[]{:S(2)}) collective-permute-start(bf16[512,512]{1,0:T(8,128)(2,1)S(1)} %get-tuple-element.12.high_ref), channel_id=1, source_target_pairs={{0,1},{1,2},{2,3},{3,4},{4,5},{5,6},{6,7},{8,9},{9,10},{10,11},{11... | collective-permute-start | bytes 1572872 | tf_op jit(solution)/shard_map/ppermute | solution.py:352
